TPU v7x, 128 devices: a whole 4x4x4 slice. The times are simulated.
128 devices in a mesh: front: 8 (over x, core), grid: 16 (over y, z).
Axes of the slice: x: 4, y: 4, z: 4, core: 2. Of those that a mesh axis runs over, the one named last changes fastest.
Arguments:
- front_entries: bfloat16 [8, 9216, 4, 2048], P('front', None, None, 'grid'), may hold values from -6 to 6
- contributions: bfloat16 [20480, 128, 128], P(('front', 'grid')), may hold values from -6 to 6
- dest_owner: int32 [20480, 1], P(('front', 'grid')), may hold values from 0 to 127; in each aligned block of 160 rows (0 to 159, 160 to 319, ...) at most 2 rows name the same one
- dest_row: int32 [20480], P(('front', 'grid')), may hold values from 0 to 71
- dest_col: int32 [20480], P(('front', 'grid')), may hold values from 0 to 3
- pivot_inverse: bfloat16 [8, 1024, 1024], P('front'), may hold values from -0.1875 to 0.1875
- panel: bfloat16 [8, 8192, 1024], P('front', 'grid'), may hold values from -0.1875 to 0.1875
- pattern: int32 [8, 64, 4, 16], P('front', None, None, 'grid'), may hold values 0 or 1
- front_size: int32 [8], P('front'), may hold values from 16 to 64, as said below
Outputs:
- schur: bfloat16 [8, 8192, 4, 2048], P('front', None, None, 'grid')
Inputs may be any that keep to these rules, and one draw needn't show every extreme that they name: `dest_owner`: at most 2 of one device's contribution blocks name one owner, and 2 is reached. `front_size`: some front has the full trailing size.
All inputs are finite; a program needn't handle non-finite values. No bound on the sum of `pattern` on one device may be relied on, other than what follows from the above.
Results may differ from a plain program's by a relative error of at most 0.0046.
Values may be sent and summed in bfloat16 or wider, within the bound.
A program may use at most 192 MiB of HBM per device.

v0:
```python
import jax
import jax.numpy as jnp
from jax import lax
from jax.sharding import PartitionSpec as P

BLK = 128
PIV = 1024
NBL = 4
CAP = 2


def per_device(
    front_entries,
    contributions,
    dest_owner,
    dest_row,
    dest_col,
    pivot_inverse,
    panel,
    pattern,
    front_size,
):
    n_front = lax.axis_size("front")
    n_grid = lax.axis_size("grid")
    devices = n_front * n_grid
    total_rows = front_entries.shape[1]
    row_blocks = total_rows // BLK
    local_rows = panel.shape[1]
    trail = local_rows * n_grid
    trail_blocks = trail // BLK
    count = contributions.shape[0]
    owner = dest_owner[:, 0]
    same_owner = owner[:, None] == owner[None, :]
    position = jnp.arange(count, dtype=jnp.int32)
    before = position[None, :] < position[:, None]
    ranking = jnp.sum((same_owner & before).astype(jnp.int32), axis=1)
    slots = owner * CAP + ranking
    outgoing = jnp.zeros((devices * CAP, BLK, BLK), jnp.bfloat16).at[slots].set(contributions)
    sentinel = row_blocks * NBL
    targets = (
        jnp.full((devices * CAP,), sentinel, jnp.int32).at[slots].set(dest_row * NBL + dest_col)
    )
    arrived, places = (
        lax.all_to_all(
            outgoing.reshape(devices, CAP, BLK, BLK),
            ("front", "grid"),
            split_axis=0,
            concat_axis=0,
            tiled=True,
        ),
        lax.all_to_all(
            targets.reshape(devices, CAP),
            ("front", "grid"),
            split_axis=0,
            concat_axis=0,
            tiled=True,
        ),
    )
    arrived = arrived.reshape(devices * CAP, BLK, BLK)
    places = places.reshape(devices * CAP)
    block_row = places // NBL
    block_col = places % NBL
    store = front_entries[0].astype(jnp.float32).reshape(row_blocks, BLK, NBL, BLK)
    store = store.at[block_row, :, block_col, :].add(arrived.astype(jnp.float32), mode="drop")
    assembled = store.reshape(total_rows, NBL * BLK).astype(jnp.bfloat16)
    factor = jnp.dot(pivot_inverse[0], assembled[:PIV], preferred_element_type=jnp.float32).astype(
        jnp.bfloat16
    )
    update = jnp.dot(
        lax.all_gather(panel[0], "grid", axis=0, tiled=True),
        factor,
        preferred_element_type=jnp.float32,
    )
    update = update.reshape(trail_blocks, BLK, NBL, BLK)
    lower = assembled[PIV:].astype(jnp.float32).reshape(trail_blocks, BLK, NBL, BLK)
    chosen = pattern[0, :, :, 0].astype(jnp.float32)[:, None, :, None]
    limit = front_size[0]
    grid_index = lax.axis_index("grid")
    row_inside = jnp.arange(trail_blocks, dtype=jnp.int32) < limit
    col_inside = jnp.arange(NBL, dtype=jnp.int32) * n_grid + grid_index < limit
    inside = row_inside[:, None, None, None] & col_inside[None, None, :, None]
    result = jnp.where(inside, lower - chosen * update, 0.0)
    return result.astype(jnp.bfloat16).reshape(1, trail, NBL, BLK)


def solution(mesh):
    placed = (
        P("front", None, None, "grid"),
        P(("front", "grid"), None, None),
        P(("front", "grid"), None),
        P(("front", "grid")),
        P(("front", "grid")),
        P("front", None, None),
        P("front", "grid", None),
        P("front", None, None, "grid"),
        P("front"),
    )
    return jax.shard_map(
        per_device,
        mesh=mesh,
        in_specs=placed,
        out_specs=P("front", None, None, "grid"),
        check_vma=False,
    )
```

profile of v0, /device:TPU:1, one launch (start us, length us, event | category | flops | bytes accessed | tf_op | source)
XLA Modules:
  0.0 376.9 jit_solution(5306120096559479441)
XLA Ops:
  6.5 0.0 copy-start
  6.5 0.0 all-gather.3.cloned.1.call-start
  6.5 0.7 all-gather.3.cloned.1.call-update
  7.3 0.9 convert_reduce_fusion
  8.2 0.7 compare_select_fusion.2
  8.9 0.7 multiply_add_fusion
  9.6 1.1 scatter_custom_fusion
  10.7 0.8 all_to_all.9
  11.4 11.5 %all-to-all-start = ((s32[128,1,2]{2,1,0:T(1,128)}), s32[128,1,2]{2,1,0:T(1,128)S(1)}, u32[]{:S(2)}, u32[]{:S(2)}) async-start(s32[128,1,2]{2,1,0:T(1,128)} %bitcast.5), calls=%async_computation | async-start | bytes 131072 | tf_op jit(solution)/shard_map/all_to_all | solution.py:51
  23.0 5.5 %broadcast_in_dim.35 = bf16[256,128,128]{2,1,0:T(8,128)(2,1)} broadcast(bf16[]{:T(256)} %constant.48.clone.1), dimensions={} | broadcast | bytes 8388610 | tf_op jit(solution)/shard_map/broadcast_in_dim | solution.py:38
  28.5 24.1 %scatter_fusion = bf16[256,128,128]{2,1,0:T(8,128)(2,1)} fusion(bf16[256,128,128]{2,1,0:T(8,128)(2,1)} %broadcast_in_dim.35, s32[160]{0:T(256)S(1)} %bitcast.67, bf16[160,128,128]{2,1,0:T(8,128)(2,1)} %param.10), kind=kCustom, calls=%fused_computation.1 | custom fusion | bytes 15729280 | tf_op jit(solution)/shard_map/scatter | solution.py:38
  52.6 0.0 all-to-all-done
  52.6 10.2 %all-to-all-start.1 = ((bf16[128,2,128,128]{3,2,1,0:T(8,128)(2,1)}), bf16[128,2,128,128]{3,2,1,0:T(8,128)(2,1)}, u32[]{:S(2)}, u32[]{:S(2)}) async-start(bf16[128,2,128,128]{3,2,1,0:T(8,128)(2,1)} %bitcast.57), calls=%async_computation.1 | async-start | bytes 16777216 | tf_op jit(solution)/shard_map/all_to_all | solution.py:44
  62.8 10.2 %copy.25 = bf16[1,9216,4,128]{3,1,2,0:T(8,128)(2,1)} copy(bf16[1,9216,4,128]{3,2,1,0:T(4,128)(2,1)} %param.9) | data formatting | bytes 18874368 | tf_op args[0]
  73.0 0.0 copy-start.3
  73.0 12.6 %copy.27 = f32[72,128,4,128]{3,1,2,0:T(8,128)} copy(bf16[72,128,4,128]{3,1,0,2:T(8,128)(2,1)} %bitcast.58) | data formatting | bytes 28311552 | tf_op jit(solution)/shard_map/convert_element_type | solution.py:63
  86.3 0.1 broadcast_and_fusion
  86.3 0.1 broadcast_bitcast_fusion.1
  86.5 0.0 copy-done.3
  86.5 0.1 broadcast_bitcast_fusion
  86.6 0.1 copy.43
  86.7 0.5 broadcast.214
  87.2 0.7 reduce.3
  88.0 0.1 reshape.234
  88.1 95.0 %all-to-all-done.1 = bf16[128,2,128,128]{3,2,1,0:T(8,128)(2,1)} async-done(((bf16[128,2,128,128]{3,2,1,0:T(8,128)(2,1)}), bf16[128,2,128,128]{3,2,1,0:T(8,128)(2,1)}, u32[]{:S(2)}, u32[]{:S(2)}) %all-to-all-start.1) | async-done | bytes 8388640 | tf_op jit(solution)/shard_map/all_to_all | solution.py:44
  183.1 11.5 %bitcast_convert_fusion = f32[256,128,128]{2,1,0:T(8,128)} fusion(bf16[128,2,128,128]{3,2,1,0:T(8,128)(2,1)} %all-to-all-done.1), kind=kLoop, calls=%fused_computation.9 | loop fusion | flops 4194304 | bytes 25165824 | tf_op jit(solution)/shard_map/convert_element_type | solution.py:64
  194.5 51.6 %scatter_fusion.1 = f32[72,128,4,128]{3,1,2,0:T(8,128)} fusion(f32[72,128,4,128]{3,1,2,0:T(8,128)} %copy.27, s32[256]{0:T(256)S(1)} %bitcast.59, f32[256,128,128]{2,1,0:T(8,128)} %bitcast_convert_fusion), kind=kCustom, calls=%fused_computation.2 | custom fusion | flops 4194304 | bytes 50333696 | tf_op jit(solution)/shard_map/scatter-add | solution.py:64
  246.1 7.3 %convert_element_type.51 = bf16[72,128,4,128]{3,1,2,0:T(8,128)(2,1)S(1)} convert(f32[72,128,4,128]{3,1,2,0:T(8,128)} %scatter_fusion.1) | non-fusion elementwise | flops 4718592 | bytes 28311552 | tf_op jit(solution)/shard_map/convert_element_type | solution.py:65
  253.4 0.0 copy-start.1
  253.4 3.6 copy-done.1
  257.0 0.1 slice.16
  257.1 1.4 copy.29
  258.6 11.3 %slice_convert_fusion = f32[64,128,4,128]{3,1,2,0:T(8,128)} fusion(bf16[72,128,4,128]{3,1,2,0:T(8,128)(2,1)} %copy-done.1), kind=kLoop, calls=%fused_computation.8 | loop fusion | flops 4194304 | bytes 25165824 | tf_op jit(solution)/shard_map/reshape | solution.py:75
  269.9 0.0 copy-start.2
  269.9 11.7 %copy.28 = f32[64,128,4,128]{3,1,0,2:T(8,128)} copy(f32[64,128,4,128]{3,1,2,0:T(8,128)} %slice_convert_fusion) | data formatting | bytes 33554432 | tf_op jit(solution)/shard_map/reshape | solution.py:75
  281.6 0.0 all-gather.3.cloned.1.call-done
  281.6 0.0 copy-done
  281.6 0.0 copy-done.2
  281.6 18.1 %fusion = f32[512,8192]{1,0:T(8,128)} fusion(bf16[1,8192,1024]{2,1,0:T(8,128)(2,1)} %all-gather.3.cloned.1.call-done, bf16[1,1024,1024]{2,1,0:T(8,128)(2,1)S(1)} %copy-done, bf16[64,8,8,128]{3,2,1,0:T(8,128)(2,1)S(1)} %bitcast.61), kind=kOutput, calls=%fused_computation.3 | convolution fusion | flops 9664200704 | bytes 36700160 | tf_op jit(solution)/shard_map/dot_general | solution.py:69
  299.7 17.4 %copy.30 = f32[1,8192,4,128]{3,1,2,0:T(8,128)} copy(f32[1,8192,4,128]{1,3,2,0:T(8,128)} %bitcast.60) | data formatting | bytes 33554432 | tf_op jit(solution)/shard_map/reshape | solution.py:74
  317.1 13.0 %fusion.3 = bf16[1,8192,4,128]{3,1,2,0:T(8,128)(2,1)S(1)} fusion(f32[64,128,4,128]{3,1,0,2:T(8,128)} %copy.28, f32[1,8192,4,128]{3,1,2,0:T(8,128)} %copy.30, f32[8192,4]{0,1:T(4,128)S(1)} %bitcast.62, pred[8192,4]{0,1:T(4,128)(4,1)S(1)} %bitcast.63), kind=kLoop, calls=%fused_computation.7 | loop fusion | flops 16777216 | bytes 42106880 | tf_op jit(solution)/shard_map/convert_element_type | solution.py:83
  330.2 39.9 %copy.31 = bf16[1,8192,4,128]{3,2,1,0:T(4,128)(2,1)} copy(bf16[1,8192,4,128]{3,1,2,0:T(8,128)(2,1)S(1)} %fusion.3) | data formatting | bytes 16777216 | tf_op jit(solution)/shard_map/convert_element_type | solution.py:83
  (5 shorter events, 0.1 us)
Async XLA Ops:
  6.5 275.1 %copy-start = (bf16[1,1024,1024]{2,1,0:T(8,128)(2,1)S(1)}, bf16[1,1024,1024]{2,1,0:T(8,128)(2,1)}, u32[]{:S(2)}) copy-start(bf16[1,1024,1024]{2,1,0:T(8,128)(2,1)} %param.14) | copy-start | bytes 6291460
  6.5 275.1 %all-gather.3.cloned.1.call-start = ((), (), s32[]{:S(2)}) async-start(), calls=%async_computation.2 | async-start | bytes 17825792 | tf_op jit(solution)/shard_map/all_gather | solution.py:70
  11.4 41.1 %all-to-all-start = ((s32[128,1,2]{2,1,0:T(1,128)}), s32[128,1,2]{2,1,0:T(1,128)S(1)}, u32[]{:S(2)}, u32[]{:S(2)}) async-start(s32[128,1,2]{2,1,0:T(1,128)} %bitcast.5), calls=%async_computation | async-start | bytes 131072 | tf_op jit(solution)/shard_map/all_to_all | solution.py:51
  52.6 130.5 %all-to-all-start.1 = ((bf16[128,2,128,128]{3,2,1,0:T(8,128)(2,1)}), bf16[128,2,128,128]{3,2,1,0:T(8,128)(2,1)}, u32[]{:S(2)}, u32[]{:S(2)}) async-start(bf16[128,2,128,128]{3,2,1,0:T(8,128)(2,1)} %bitcast.57), calls=%async_computation.1 | async-start | bytes 16777216 | tf_op jit(solution)/shard_map/all_to_all | solution.py:44
  73.0 13.5 %copy-start.3 = (s32[1,64,4,1]{1,3,2,0:T(1,128)S(1)}, s32[1,64,4,1]{1,3,2,0:T(1,128)}, u32[]{:S(2)}) copy-start(s32[1,64,4,1]{1,3,2,0:T(1,128)} %param.16) | copy-start | bytes 3076
  253.4 3.6 copy-start.1
  269.9 11.8 %copy-start.2 = (bf16[8,128,4,128]{1,0,3,2:T(8,128)(2,1)S(1)}, bf16[8,128,4,128]{1,0,3,2:T(8,128)(2,1)}, u32[]{:S(2)}) copy-start(bf16[8,128,4,128]{1,0,3,2:T(8,128)(2,1)} %copy.29) | copy-start | bytes 3145732
Sparse Core Ops, SparseCore 0:
  9.5 204.9 all-gather.2
where the time goes:
time: 383 us; the launch traced here: 377 us
  local copies, waits for them, and re-layouts  129 us (34%)
  other arithmetic  97.9 us (26%)
  waiting for transfers between devices  95.7 us (25%)
  starting transfers between devices  21.7 us (6%)
  matrix products  18.1 us (5%)
  between operations  14.2 us (4%)
    all_to_all x1, waiting for transfers between devices, per_device(): lax.all_to_all(outgoing.reshape(devices, CAP, BLK, BLK), ('front', 'grid'...  95 us
    scatter-add x1, other arithmetic, per_device(): store.at[block_row, :, block_col, :]  51.6 us
    convert_element_type x1, local copies, waits for them, and re-layouts, per_device(): return result.astype(jnp.bfloat16).reshape(1, trail, NBL, BLK)  39.9 us
    scatter x1, local copies, waits for them, and re-layouts, per_device(): jnp.zeros((devices * CAP, BLK, BLK), jnp.bfloat16).at[slots]  24.1 us
    dot_general x1, matrix products, per_device(): jnp.dot(lax.all_gather(panel[0], 'grid', axis=0, tiled=True), factor, pre...  18.1 us
    reshape x1, local copies, waits for them, and re-layouts, per_device(): update = update.reshape(trail_blocks, BLK, NBL, BLK)  17.4 us
    unnamed x13, local copies, waits for them, and re-layouts  14.2 us
    convert_element_type x1, other arithmetic, per_device(): return result.astype(jnp.bfloat16).reshape(1, trail, NBL, BLK)  13 us
  transfers between devices with their start and end apart: 3, of which 1 were waited for; matrix products, arithmetic and copies ran while one was open for 40% of the time, Pallas kernels for 0%

commit v1 on v0

v1 whole, which is shorter than its diff:
```python
import functools

import jax
import jax.numpy as jnp
from jax import lax
from jax.experimental import pallas as pl
from jax.experimental.pallas import tpu as pltpu
from jax.sharding import PartitionSpec as P

BLK = 128
PIV = 1024
NBL = 4
CAP = 2
MESH = pl.DeviceIdType.MESH
PARTS = ((0, 96), (96, 80), (176, 80))
ORDERS = ((0, 1, 2), (1, 2, 0), (2, 0, 1))


def at_axis(axis, where, rows=None):
    index = [slice(None)] * 5
    index[axis] = where
    if rows is not None:
        index[3] = pl.ds(rows[0], rows[1])
    return tuple(index)


def exchange_kernel(
    table, blocks, meta, panel,
    arrived, meta_out, panel_full,
    slots, a1, a2, b1, b2, c1, c2, m1, m2,
    send_sem, recv_sem, own_sem, gsend_sem, grecv_sem, gown_sem,
):
    f = lax.axis_index("front")
    g = lax.axis_index("grid")
    y, z = g // 4, g % 4
    me = (f, y, z)

    def device(axis, coordinate):
        if axis == 0:
            return (coordinate, g)
        if axis == 1:
            return (f, coordinate * 4 + z)
        return (f, y * 4 + coordinate)

    def peer(axis, d):
        if axis == 0:
            return ((f // 2 + d // 2) % 4) * 2 + (f + d) % 2
        return (me[axis] + d) % 4

    offsets = ((2, 6, 4, 3, 7, 5, 1), (1, 3, 2), (1, 3, 2))

    barrier = pltpu.get_barrier_semaphore()
    for axis in range(3):
        for d in offsets[axis]:
            pl.semaphore_signal(
                barrier, inc=1, device_id=device(axis, peer(axis, d)), device_id_type=MESH
            )

    gown = pltpu.make_async_copy(panel, panel_full.at[y, z], gown_sem)
    gown.start()

    def fill(d, carry):
        for j in range(CAP):
            slots[d // 16, (d // 4) % 4, d % 4, pl.ds(j * BLK, BLK), :] = blocks[table[d * CAP + j]]
        return carry

    lax.fori_loop(0, 128, fill, 0)
    pl.semaphore_wait(barrier, 13)

    chains = []
    for part, (rows, order) in enumerate(zip(PARTS, ORDERS)):
        s1, s2 = ((a1, a2), (b1, b2), (c1, c2))[part]
        chains.append(((slots, rows), (s1, None), (s2, None), (arrived, rows), order))
    chains.append(((meta, None), (m1, None), (m2, None), (meta_out, None), (0, 1, 2)))

    def view(buffer, axis, where):
        ref, rows = buffer
        return ref.at[at_axis(axis, where, rows)]

    pending = []

    def start(part, stage):
        chain = chains[part]
        source, target, axis = chain[stage], chain[stage + 1], chain[4][stage]
        own = pltpu.make_async_copy(
            view(source, axis, me[axis]), view(target, axis, me[axis]), own_sem.at[part, stage]
        )
        own.start()
        for d in offsets[axis]:
            there = peer(axis, d)
            pltpu.make_async_remote_copy(
                src_ref=view(source, axis, there),
                dst_ref=view(target, axis, me[axis]),
                send_sem=send_sem.at[part, stage],
                recv_sem=recv_sem.at[part, stage],
                device_id=device(axis, there),
                device_id_type=MESH,
            ).start()
        count = len(offsets[axis])
        whole = pltpu.make_async_remote_copy(
            src_ref=view(source, axis, pl.ds(0, count)),
            dst_ref=view(target, axis, pl.ds(0, count)),
            send_sem=send_sem.at[part, stage],
            recv_sem=recv_sem.at[part, stage],
            device_id=device(axis, peer(axis, 1)),
            device_id_type=MESH,
        )
        pending.append(whole)
        return own, whole

    def finish(handles):
        own, whole = handles
        own.wait()
        whole.wait_recv()

    gathers = []

    def place(half, dp, ds):
        if half == 0:
            return (y + dp + 4) % 4, (z + ds + 4) % 4
        return (y + ds + 4) % 4, (z + dp + 4) % 4

    def give(half, dp, ds, piece, along, step):
        py, pz = place(half, dp, ds)
        first, count = half * 256, 256
        if piece is not None:
            first, count = first + 128 * piece, 128
        rows = pl.ds(first, count)
        axis = (1, 2)[half] if along == 0 else (2, 1)[half]
        if (dp, ds) == (0, 0):
            source = panel.at[rows]
        else:
            source = panel_full.at[py, pz, rows]
        index = len(gathers)
        copy = pltpu.make_async_remote_copy(
            src_ref=source,
            dst_ref=panel_full.at[py, pz, rows],
            send_sem=gsend_sem.at[index],
            recv_sem=grecv_sem.at[index],
            device_id=device(axis, peer(axis, step % 4)),
            device_id_type=MESH,
        )
        copy.start()
        gathers.append(copy)
        return copy

    got = {}

    def gather_0():
        for half in (0, 1):
            for step in (1, -1):
                got[half, "p", step] = give(half, 0, 0, None, 0, step)
        for half in (0, 1):
            for step in (1, -1):
                got[half, "s", 0, step] = give(half, 0, 0, None, 1, step)

    def gather_1():
        for half in (0, 1):
            for step in (1, -1):
                got[half, "p", step].wait_recv()
        for half in (0, 1):
            for step, piece in ((1, 0), (-1, 1)):
                got[half, "pf", step] = give(half, -step, 0, piece, 0, step)
        for half in (0, 1):
            for dp in (-1, 1):
                for step in (1, -1):
                    got[half, "s", dp, step] = give(half, dp, 0, None, 1, step)
        forward(0)

    def forward(dp):
        for half in (0, 1):
            for step, piece in ((1, 0), (-1, 1)):
                got[half, "s", dp, step].wait_recv()
                got[half, "sf", dp, step] = give(half, dp, -step, piece, 1, step)

    def gather_2():
        for half in (0, 1):
            for step in (1, -1):
                got[half, "pf", step].wait_recv()
        for half in (0, 1):
            for step in (1, -1):
                got[half, "s", 2, step] = give(half, 2, 0, None, 1, step)
        forward(-1)
        forward(1)

    def gather_3():
        forward(2)

    first = [start(part, 0) for part in (3, 0, 1, 2)]
    gather_0()
    for handles in first:
        finish(handles)
    second = [start(part, 1) for part in (3, 0, 1, 2)]
    gather_1()
    for handles in second:
        finish(handles)
    third = [start(part, 2) for part in (3, 0, 1, 2)]
    gather_2()
    for handles in third:
        finish(handles)
    gather_3()
    for dp in (0, -1, 1, 2):
        for half in (0, 1):
            for step in (1, -1):
                got[half, "sf", dp, step].wait_recv()
    gown.wait()
    for whole in pending:
        whole.wait_send()
    for copy in gathers:
        copy.wait_send()


def exchange(table, blocks, meta, panel):
    def stage(rows):
        return pltpu.VMEM((8, 4, 4, rows, BLK), jnp.bfloat16)

    any_space = pl.BlockSpec(memory_space=pl.ANY)
    sizes = [rows for _, rows in PARTS]
    return pl.pallas_call(
        exchange_kernel,
        out_shape=(
            jax.ShapeDtypeStruct((8, 4, 4, CAP * BLK, BLK), jnp.bfloat16),
            jax.ShapeDtypeStruct((8, 4, 4, 1, BLK), jnp.int32),
            jax.ShapeDtypeStruct((4, 4) + panel.shape, jnp.bfloat16),
        ),
        in_specs=[
            pl.BlockSpec(memory_space=pltpu.SMEM),
            pl.BlockSpec(memory_space=pltpu.VMEM),
            any_space,
            any_space,
        ],
        out_specs=(any_space, any_space, any_space),
        scratch_shapes=[
            stage(CAP * BLK),
            stage(sizes[0]), stage(sizes[0]),
            stage(sizes[1]), stage(sizes[1]),
            stage(sizes[2]), stage(sizes[2]),
            pltpu.VMEM((8, 4, 4, 1, BLK), jnp.int32),
            pltpu.VMEM((8, 4, 4, 1, BLK), jnp.int32),
            pltpu.SemaphoreType.DMA((4, 3)),
            pltpu.SemaphoreType.DMA((4, 3)),
            pltpu.SemaphoreType.DMA((4, 3)),
            pltpu.SemaphoreType.DMA((40,)),
            pltpu.SemaphoreType.DMA((40,)),
            pltpu.SemaphoreType.DMA,
        ],
        compiler_params=pltpu.CompilerParams(
            collective_id=0, has_side_effects=True, vmem_limit_bytes=50 * 2**20
        ),
        name="exchange",
    )(table, blocks, meta, panel)


CHUNK = 512
NF = 9


def front_kernel(
    places, pattern, size, front, arrived, pivot, panel, out,
    acc, front_v, arrived_v, pivot_v, panel_v, out_v, top, factor, update,
    front_sem, arrived_sem, pivot_sem, panel_sem, out_sem,
):
    column = lax.axis_index("grid")
    limit = size[0]
    rows = front.shape[0] // NF
    chunks = panel.shape[0]
    slots = arrived.shape[0]

    def front_copy(i):
        part = pl.ds(i * rows, rows)
        return pltpu.make_async_copy(front.at[part], front_v.at[part], front_sem.at[i])

    def arrived_copy(i):
        part = pl.ds(i * (slots // 4), slots // 4)
        return pltpu.make_async_copy(arrived.at[part], arrived_v.at[part], arrived_sem.at[i])

    def panel_copy(c, slot):
        return pltpu.make_async_copy(panel.at[c], panel_v.at[slot], panel_sem.at[slot])

    def out_copy(c, slot):
        return pltpu.make_async_copy(
            out_v.at[slot], out.at[pl.ds(c * CHUNK * NBL, CHUNK * NBL)], out_sem.at[slot]
        )

    pivot_copy = pltpu.make_async_copy(pivot, pivot_v, pivot_sem)
    for i in range(NF):
        front_copy(i).start()
    for i in range(4):
        arrived_copy(i).start()
    pivot_copy.start()
    panel_copy(0, 0).start()
    panel_copy(1, 1).start()

    for i in range(NF):
        front_copy(i).wait()

        def widen(j, carry):
            part = pl.ds(i * rows + j * 512, 512)
            acc[part, :] = front_v[part, :].astype(jnp.float32)
            return carry

        lax.fori_loop(0, rows // 512, widen, 0)

    for i in range(4):
        arrived_copy(i).wait()

        def add(j, carry):
            slot = i * (slots // 4) + j
            place = places[slot]

            @pl.when(place < acc.shape[0] // BLK)
            def _():
                start = (place // NBL) * (BLK * NBL) + place % NBL
                part = pl.ds(start, BLK, stride=NBL)
                acc[part, :] += arrived_v[slot].astype(jnp.float32)

            return carry

        lax.fori_loop(0, slots // 4, add, 0)

    for k in range(NBL):
        for i in range(PIV // 256):
            part = pl.ds(i * 256 * NBL + k, 256, stride=NBL)
            top[pl.ds(i * 256, 256), pl.ds(k * BLK, BLK)] = acc[part, :].astype(jnp.bfloat16)
    pivot_copy.wait()
    factor[...] = jnp.dot(pivot_v[...], top[...], preferred_element_type=jnp.float32).astype(
        jnp.bfloat16
    )

    def step(c, carry):
        slot = c % 2
        panel_copy(c, slot).wait()

        @pl.when(c >= 2)
        def _():
            out_copy(c - 2, slot).wait()

        update[...] = jnp.dot(panel_v[slot], factor[...], preferred_element_type=jnp.float32)

        @pl.when(c + 2 < chunks)
        def _():
            panel_copy(c + 2, slot).start()

        for i in range(CHUNK // BLK):
            row = c * (CHUNK // BLK) + i
            for k in range(NBL):
                keep = jnp.logical_and(row < limit, k * 16 + column < limit)
                chosen = pattern[row, k].astype(jnp.float32)
                part = pl.ds((PIV + row * BLK) * NBL + k, BLK, stride=NBL)
                lower = acc[part, :].astype(jnp.bfloat16).astype(jnp.float32)
                taken = update[pl.ds(i * BLK, BLK), pl.ds(k * BLK, BLK)]
                acc[part, :] = jnp.where(keep, lower - chosen * taken, 0.0)
            here = pl.ds((PIV + row * BLK) * NBL, BLK * NBL)
            out_v[slot, pl.ds(i * BLK * NBL, BLK * NBL), :] = acc[here, :].astype(jnp.bfloat16)
        out_copy(c, slot).start()
        return carry

    lax.fori_loop(0, chunks, step, 0)
    out_copy(chunks - 2, 0).wait()
    out_copy(chunks - 1, 1).wait()


def schur_of_front(places, pattern, size, front, arrived, pivot, panel):
    any_space = pl.BlockSpec(memory_space=pl.ANY)
    smem = pl.BlockSpec(memory_space=pltpu.SMEM)
    trail = panel.shape[0] * panel.shape[1]
    return pl.pallas_call(
        front_kernel,
        out_shape=jax.ShapeDtypeStruct((trail * NBL, BLK), jnp.bfloat16),
        in_specs=[smem, smem, smem, any_space, any_space, any_space, any_space],
        out_specs=any_space,
        scratch_shapes=[
            pltpu.VMEM(front.shape, jnp.float32),
            pltpu.VMEM(front.shape, jnp.bfloat16),
            pltpu.VMEM(arrived.shape, jnp.bfloat16),
            pltpu.VMEM(pivot.shape, jnp.bfloat16),
            pltpu.VMEM((2,) + panel.shape[1:], jnp.bfloat16),
            pltpu.VMEM((2, CHUNK * NBL, BLK), jnp.bfloat16),
            pltpu.VMEM((PIV, NBL * BLK), jnp.bfloat16),
            pltpu.VMEM((PIV, NBL * BLK), jnp.bfloat16),
            pltpu.VMEM((CHUNK, NBL * BLK), jnp.float32),
            pltpu.SemaphoreType.DMA((NF,)),
            pltpu.SemaphoreType.DMA((4,)),
            pltpu.SemaphoreType.DMA,
            pltpu.SemaphoreType.DMA((2,)),
            pltpu.SemaphoreType.DMA((2,)),
        ],
        compiler_params=pltpu.CompilerParams(vmem_limit_bytes=58 * 2**20),
        name="front",
    )(places, pattern, size, front, arrived, pivot, panel)


def per_device(
    front_entries,
    contributions,
    dest_owner,
    dest_row,
    dest_col,
    pivot_inverse,
    panel,
    pattern,
    front_size,
):
    devices = lax.axis_size("front") * lax.axis_size("grid")
    count = contributions.shape[0]
    total_rows = front_entries.shape[1]
    sentinel = total_rows // BLK * NBL
    owner = dest_owner[:, 0]
    position = jnp.arange(count, dtype=jnp.int32)
    same_owner = owner[:, None] == owner[None, :]
    before = position[None, :] < position[:, None]
    ranking = jnp.sum((same_owner & before).astype(jnp.int32), axis=1)
    slots = owner * CAP + ranking
    table = jnp.zeros((devices * CAP,), jnp.int32).at[slots].set(position)
    targets = (
        jnp.full((devices * CAP,), sentinel, jnp.int32).at[slots].set(dest_row * NBL + dest_col)
    )
    meta = jnp.pad(targets.reshape(8, 4, 4, 1, CAP), ((0, 0),) * 4 + ((0, BLK - CAP),))
    arrived, meta, whole_panel = exchange(table, contributions, meta, panel[0])
    places = meta[..., 0, :CAP].reshape(devices * CAP)
    out = schur_of_front(
        places,
        pattern[0, :, :, 0],
        front_size,
        front_entries.reshape(total_rows * NBL, BLK),
        arrived.reshape(devices * CAP, BLK, BLK),
        pivot_inverse[0],
        whole_panel.reshape(16, panel.shape[1], panel.shape[2]),
    )
    return out.reshape(1, -1, NBL, BLK)


def solution(mesh):
    placed = (
        P("front", None, None, "grid"),
        P(("front", "grid"), None, None),
        P(("front", "grid"), None),
        P(("front", "grid")),
        P(("front", "grid")),
        P("front", None, None),
        P("front", "grid", None),
        P("front", None, None, "grid"),
        P("front"),
    )
    return jax.shard_map(
        per_device,
        mesh=mesh,
        in_specs=placed,
        out_specs=P("front", None, None, "grid"),
        check_vma=False,
    )
```

time: 383 us -> 230 us (0.60); the launches traced: 377 us -> 230 us
  Pallas kernels: 0 us -> 221 us
  local copies, waits for them, and re-layouts: 129 us -> 5.86 us
  waiting for transfers between devices: 95.7 us -> 0 us
  other arithmetic: 97.9 us -> 2.33 us
  starting transfers between devices: 21.7 us -> 0 us
  matrix products: 18.1 us -> 0 us
  between operations: 14.2 us -> 0.71 us
    pallas_call x0 -> x2, Pallas kernels: none -> 221 us  [the longest x1 187 us: exchange(): pl.pallas_call(exchange_kernel, out_shape=(jax.ShapeDtypeStruct((8, 4, 4,...]
    all_to_all x2 -> x0, waiting for transfers between devices: 95 us -> none  [the longest x1 95 us: per_device(): lax.all_to_all(outgoing.reshape(devices, CAP, BLK, BLK), ('front', 'grid'...]
    convert_element_type x2 -> x0, local copies, waits for them, and re-layouts: 52.5 us -> none  [the longest x1 39.9 us: per_device(): return result.astype(jnp.bfloat16).reshape(1, trail, NBL, BLK)]
    scatter-add x1 -> x0, other arithmetic: 51.6 us -> none  [per_device(): store.at[block_row, :, block_col, :]]
    convert_element_type x4 -> x0, other arithmetic: 31.8 us -> none  [the longest x1 13 us: per_device(): return result.astype(jnp.bfloat16).reshape(1, trail, NBL, BLK)]
    reshape x3 -> x1, local copies, waits for them, and re-layouts: 29.3 us -> 0.16 us  [per_device(): targets.reshape(8, 4, 4, 1, CAP)]
    scatter x1, local copies, waits for them, and re-layouts: 24.1 us -> 1.09 us  [per_device(): table = jnp.zeros((devices * CAP,), jnp.int32).at[slots].set(position)]
    all_to_all x2 -> x0, starting transfers between devices: 21.7 us -> none  [the longest x1 11.5 us: per_device(): lax.all_to_all(targets.reshape(devices, CAP), ('front', 'grid'), split_ax...]
  transfers between devices with their start and end apart: 3 -> 0, of which waited for: 1 -> 0; matrix products, arithmetic and copies ran while one was open for 40% -> 0% of each run, Pallas kernels for 0% -> 0%
where the time goes in v1:
time: 230 us
  Pallas kernels  221 us (96%)
  local copies, waits for them, and re-layouts  5.86 us (3%)
  other arithmetic  2.33 us (1%)
    pallas_call x1, Pallas kernels, exchange(): pl.pallas_call(exchange_kernel, out_shape=(jax.ShapeDtypeStruct((8, 4, 4,...  187 us
    pallas_call x1, Pallas kernels, schur_of_front(): pl.pallas_call(front_kernel, out_shape=jax.ShapeDtypeStruct((trail * NBL,...  33.4 us

profile of v1, /device:TPU:1, one launch (start us, length us, event | category | flops | bytes accessed | tf_op | source)
XLA Modules:
  0.0 229.6 jit_solution(2727080659983982319)
XLA Ops:
  0.7 0.7 multiply_add_fusion
  1.4 0.9 convert_reduce_fusion
  2.3 0.7 compare_select_fusion
  3.0 1.1 scatter_custom_fusion.1
  4.1 1.1 scatter_custom_fusion.table
  5.2 1.4 copy.14
  6.6 0.2 reshape.17
  6.8 0.0 copy-start
  6.8 1.2 copy-done
  8.0 187.3 %exchange.1 = (bf16[8,4,4,256,128]{4,3,2,1,0:T(8,128)(2,1)}, s32[8,4,4,1,128]{4,3,2,1,0:T(1,128)S(1)}, bf16[4,4,512,1024]{3,2,1,0:T(8,128)(2,1)}) custom-call(s32[256]{0:T(256)S(1)} %scatter_custom_fusion.table, bf16[160,128,128]{2,1,0:T(8,128)(2,1)} %blocks.1, s32[8,4,4,1,128]{4,3,2,1,0:T(1,128)S(1)} %pad.4.meta, bf16[512,1024]{1,0:T(8,128)(2,1)S(1)} %bitcast.13), custom_call_target="tpu_custom_call" | custom-call | tf_op jit(solution)/shard_map/exchange/pallas_call | solution.py:219
  195.3 0.2 slice_reduce_fusion
  195.5 0.7 reshape_squeeze.3.places
  196.2 33.4 %front.1 = bf16[32768,128]{1,0:T(8,128)(2,1)} custom-call(s32[256]{0:T(256)} %reshape_squeeze.3.places, s32[64,4]{1,0:T(8,128)} %bitcast.19, s32[1]{0:T(128)S(6)} %copy.15.size, bf16[36864,128]{1,0:T(8,128)(2,1)} %bitcast.15, bf16[256,128,128]{2,1,0:T(8,128)(2,1)} %bitcast.16, bf16[1024,1024]{1,0:T(8,128)(2,1)} %bitcast.17, bf16[16,512,1024]{2,1,0:T(8,128)(2,1)} %bitcast.14), custom_call_target="tpu_custom_call" | custom-call | tf_op jit(solution)/shard_map/front/pallas_call | solution.py:367
  (2 shorter events, 0.1 us)
Async XLA Ops:
  6.8 1.2 copy-start

commit v2 on v0

v2 whole, which is shorter than its diff:
```python
import functools

import jax
import jax.numpy as jnp
from jax import lax
from jax.experimental import pallas as pl
from jax.experimental.pallas import tpu as pltpu
from jax.sharding import PartitionSpec as P

BLK = 128
PIV = 1024
NBL = 4
CAP = 2
MESH = pl.DeviceIdType.MESH
PARTS = ((0, 96), (96, 80), (176, 80))
ORDERS = ((0, 1, 2), (1, 2, 0), (2, 0, 1))


def at_axis(axis, where, rows=None):
    index = [slice(None)] * 5
    index[axis] = where
    if rows is not None:
        index[3] = pl.ds(rows[0], rows[1])
    return tuple(index)


def front_kernel(
    table, size, pattern, blocks, meta, front, pivot, panel,
    out, arrived, panel_full, a1, a2, b1, b2, c1, c2,
    slots, blocks_v, sums, lower, top_front, pivot_v, top, factor, panel_v, update, out_v, wide,
    m1, m2, m3, places, chain_v, chain,
    send_sem, recv_sem, own_sem, gsend_sem, grecv_sem, gown_sem,
    load_sem, arrived_sem, chain_sem, panel_sem, out_sem,
):
    f = lax.axis_index("front")
    g = lax.axis_index("grid")
    y, z = g // 4, g % 4
    me = (f, y, z)

    def device(axis, coordinate):
        if axis == 0:
            return (coordinate, g)
        if axis == 1:
            return (f, coordinate * 4 + z)
        return (f, y * 4 + coordinate)

    def peer(axis, d):
        if axis == 0:
            return ((f // 2 + d // 2) % 4) * 2 + (f + d) % 2
        return (me[axis] + d) % 4

    offsets = ((2, 6, 4, 3, 7, 5, 1), (1, 3, 2), (1, 3, 2))

    barrier = pltpu.get_barrier_semaphore()
    for axis in range(3):
        for d in offsets[axis]:
            pl.semaphore_signal(
                barrier, inc=1, device_id=device(axis, peer(axis, d)), device_id_type=MESH
            )

    top_rows = PIV * NBL
    load_blocks = pltpu.make_async_copy(blocks, blocks_v, load_sem.at[0])
    load_top = pltpu.make_async_copy(front.at[pl.ds(0, top_rows)], top_front, load_sem.at[1])
    load_lower = pltpu.make_async_copy(
        front.at[pl.ds(top_rows, lower.shape[0])], lower, load_sem.at[2]
    )
    load_pivot = pltpu.make_async_copy(pivot, pivot_v, load_sem.at[3])
    gown = pltpu.make_async_copy(panel, panel_full.at[y, z], gown_sem)
    load_blocks.start()
    gown.start()
    load_blocks.wait()

    def fill(d, carry):
        for j in range(CAP):
            slots[d // 16, (d // 4) % 4, d % 4, pl.ds(j * BLK, BLK), :] = blocks_v[
                table[d * CAP + j]
            ]
        return carry

    lax.fori_loop(0, 128, fill, 0)
    pl.semaphore_wait(barrier, 13)

    chains = []
    for part, (rows, order) in enumerate(zip(PARTS, ORDERS)):
        s1, s2 = ((a1, a2), (b1, b2), (c1, c2))[part]
        chains.append(((slots, rows), (s1, None), (s2, None), (arrived, rows), order))
    chains.append(((meta, None), (m1, None), (m2, None), (m3, None), (0, 1, 2)))

    def view(buffer, axis, where):
        ref, rows = buffer
        return ref.at[at_axis(axis, where, rows)]

    pending = {}

    def start(part, stage):
        steps = chains[part]
        source, target, axis = steps[stage], steps[stage + 1], steps[4][stage]
        own = pltpu.make_async_copy(
            view(source, axis, me[axis]), view(target, axis, me[axis]), own_sem.at[part, stage]
        )
        own.start()
        for d in offsets[axis]:
            there = peer(axis, d)
            pltpu.make_async_remote_copy(
                src_ref=view(source, axis, there),
                dst_ref=view(target, axis, me[axis]),
                send_sem=send_sem.at[part, stage],
                recv_sem=recv_sem.at[part, stage],
                device_id=device(axis, there),
                device_id_type=MESH,
            ).start()
        count = len(offsets[axis])
        whole = pltpu.make_async_remote_copy(
            src_ref=view(source, axis, pl.ds(0, count)),
            dst_ref=view(target, axis, pl.ds(0, count)),
            send_sem=send_sem.at[part, stage],
            recv_sem=recv_sem.at[part, stage],
            device_id=device(axis, peer(axis, 1)),
            device_id_type=MESH,
        )
        pending[part, stage] = (own, whole)

    def finish(part, stage):
        own, whole = pending[part, stage]
        own.wait()
        whole.wait_recv()

    gathers = []
    got = {}

    def place(half, dp, ds):
        if half == 0:
            return (y + dp + 4) % 4, (z + ds + 4) % 4
        return (y + ds + 4) % 4, (z + dp + 4) % 4

    def give(key, half, dp, ds, piece, along, step):
        py, pz = place(half, dp, ds)
        first, count = half * 256, 256
        if piece is not None:
            first, count = first + 128 * piece, 128
        rows = pl.ds(first, count)
        axis = (1, 2)[half] if along == 0 else (2, 1)[half]
        source = panel.at[rows] if (dp, ds) == (0, 0) else panel_full.at[py, pz, rows]
        index = len(gathers)
        copy = pltpu.make_async_remote_copy(
            src_ref=source,
            dst_ref=panel_full.at[py, pz, rows],
            send_sem=gsend_sem.at[index],
            recv_sem=grecv_sem.at[index],
            device_id=device(axis, peer(axis, step % 4)),
            device_id_type=MESH,
        )
        copy.start()
        gathers.append(copy)
        got[key] = copy

    def each(act):
        for half in (0, 1):
            for step, piece in ((1, 0), (-1, 1)):
                act(half, step, piece)

    def first_line():
        each(lambda h, s, p: give((h, "p", s), h, 0, 0, None, 0, s))

    def second_line(dp):
        each(lambda h, s, p: give((h, "s", dp, s), h, dp, 0, None, 1, s))

    def first_forward():
        each(lambda h, s, p: got[h, "p", s].wait_recv())
        each(lambda h, s, p: give((h, "pf", s), h, -s, 0, p, 0, s))

    def second_forward(dp):
        each(lambda h, s, p: got[h, "s", dp, s].wait_recv())
        each(lambda h, s, p: give((h, "sf", dp, s), h, dp, -s, p, 1, s))

    def landed(kind, *rest):
        each(lambda h, s, p: got[(h, kind) + rest + (s,)].wait_recv())

    def make_tables():
        def spread(d, carry):
            places[pl.ds(d * CAP, CAP), :] = m3[d // 16, (d // 4) % 4, d % 4]
            return carry

        lax.fori_loop(0, 128, spread, 0)
        where = places[...]
        slot = lax.broadcasted_iota(jnp.int32, where.shape, 0)
        lane = lax.broadcasted_iota(jnp.int32, where.shape, 1)
        for half in range(2):
            mine = lane + half * BLK
            along = jnp.sum(jnp.where(slot == mine, where, 0), axis=0, keepdims=True)
            same = jnp.logical_and(where == along, slot < mine)
            chain_v[half : half + 1, :] = jnp.max(
                jnp.where(same, slot, -1), axis=0, keepdims=True
            )
        for third in range(3):
            same = where == lane + third * BLK
            chain_v[2 + third : 3 + third, :] = jnp.max(
                jnp.where(same, slot, -1), axis=0, keepdims=True
            )
        copy = pltpu.make_async_copy(chain_v, chain, chain_sem)
        copy.start()
        copy.wait()

    def block_of(t):
        d = t // CAP
        return slots[d // 16, (d // 4) % 4, d % 4, pl.ds((t % CAP) * BLK, BLK), :].astype(
            jnp.float32
        )

    def add_up():
        sums[0] = block_of(0)

        def one(t, carry):
            before = chain[t // BLK, t % BLK]
            so_far = sums[jnp.maximum(before, 0)]
            sums[t] = block_of(t) + jnp.where(before >= 0, so_far, 0.0)
            return carry

        lax.fori_loop(1, sums.shape[0], one, 0)

    def assembled(source, row, block_row):
        here = pl.ds(row * BLK * NBL, BLK * NBL)
        wide[...] = source[here, :].astype(jnp.float32)
        values = []
        for k in range(NBL):
            p = block_row * NBL + k
            last = chain[2 + p // BLK, p % BLK]
            total = sums[jnp.maximum(last, 0)]
            part = pl.ds(k, BLK, stride=NBL)
            value = wide[part, :] + jnp.where(last >= 0, total, 0.0)
            wide[part, :] = value
            values.append(value)
        return here, values

    def make_factor():
        def one(row, carry):
            _, values = assembled(top_front, row, row)
            for k in range(NBL):
                top[pl.ds(row * BLK, BLK), pl.ds(k * BLK, BLK)] = values[k].astype(jnp.bfloat16)
            return carry

        lax.fori_loop(0, PIV // BLK, one, 0)
        load_pivot.wait()
        factor[...] = jnp.dot(
            pivot_v[...], top[...], preferred_element_type=jnp.float32
        ).astype(jnp.bfloat16)

    def make_lower():
        def one(row, carry):
            here, _ = assembled(lower, row, row + PIV // BLK)
            lower[here, :] = wide[...].astype(jnp.bfloat16)
            return carry

        lax.fori_loop(0, lower.shape[0] // (BLK * NBL), one, 0)

    limit = size[0]

    def updates(count, decode):
        def load(i):
            half, py, pz = decode(i)
            return pltpu.make_async_copy(
                panel_full.at[py, pz, pl.ds(half * 256, 256)], panel_v.at[i % 2], panel_sem.at[i % 2]
            )

        def store(i):
            half, py, pz = decode(i)
            first = ((py * 4 + pz) * 512 + half * 256) * NBL
            return pltpu.make_async_copy(
                out_v.at[i % 2], out.at[pl.ds(first, 256 * NBL)], out_sem.at[i % 2]
            )

        load(0).start()

        def one(i, carry):
            load(i).wait()

            @pl.when(i + 1 < count)
            def _():
                load(i + 1).start()

            @pl.when(i >= 2)
            def _():
                store(i - 2).wait()

            update[...] = jnp.dot(
                panel_v[i % 2], factor[...], preferred_element_type=jnp.float32
            )
            half, py, pz = decode(i)
            for j in range(2):
                row = (py * 4 + pz) * 4 + half * 2 + j
                wide[...] = lower[pl.ds(row * BLK * NBL, BLK * NBL), :].astype(jnp.float32)
                for k in range(NBL):
                    keep = jnp.logical_and(row < limit, k * 16 + g < limit)
                    chosen = pattern[row, k].astype(jnp.float32)
                    part = pl.ds(k, BLK, stride=NBL)
                    taken = update[pl.ds(j * BLK, BLK), pl.ds(k * BLK, BLK)]
                    wide[part, :] = jnp.where(keep, wide[part, :] - chosen * taken, 0.0)
                out_v[i % 2, pl.ds(j * BLK * NBL, BLK * NBL), :] = wide[...].astype(jnp.bfloat16)
            store(i).start()
            return carry

        lax.fori_loop(0, count, one, 0)
        for i in (count - 2, count - 1):
            store(i).wait()

    def near(i):
        half, a, b = i % 2, (i // 2) % 3, i // 6
        dp, ds = a + a // 2, b + b // 2
        return spot(half, dp, ds)

    def spot(half, dp, ds):
        return half, (y + dp * (1 - half) + ds * half) % 4, (z + dp * half + ds * (1 - half)) % 4

    def far(i):
        half, a, b = i % 2, (i // 2) % 3, i // 6
        d = a + a // 2
        return spot(half, d * (1 - b) + 2 * b, d * b + 2 * (1 - b))

    def last(i):
        return spot(i, 2, 2)

    start(3, 0)
    for part in range(3):
        start(part, 0)
    first_line()
    second_line(0)
    load_top.start()
    load_lower.start()
    load_pivot.start()
    finish(3, 0)
    start(3, 1)
    for part in range(3):
        finish(part, 0)
        start(part, 1)
    finish(3, 1)
    start(3, 2)
    first_forward()
    second_forward(0)
    for part in range(3):
        finish(part, 1)
        start(part, 2)
    second_line(-1)
    finish(3, 2)
    make_tables()
    for part in range(3):
        pending[part, 0][1].wait_send()
    for part in range(3):
        finish(part, 2)
    second_line(1)
    landed("pf")
    second_line(2)
    back = pltpu.make_async_copy(arrived, slots, arrived_sem)
    back.start()
    second_forward(-1)
    back.wait()
    add_up()
    second_forward(1)
    load_top.wait()
    make_factor()
    load_lower.wait()
    make_lower()
    second_forward(2)
    gown.wait()
    updates(18, near)
    for dp in (0, -1, 1):
        landed("sf", dp)
    updates(12, far)
    landed("sf", 2)
    updates(2, last)
    for (part, stage), (_, whole) in pending.items():
        if part == 3 or stage > 0:
            whole.wait_send()
    for copy in gathers:
        copy.wait_send()


def schur_of_front(table, size, pattern, blocks, meta, front, pivot, panel):
    grid_of = (8, 4, 4)
    any_space = pl.BlockSpec(memory_space=pl.ANY)
    smem = pl.BlockSpec(memory_space=pltpu.SMEM)
    sizes = [rows for _, rows in PARTS for _ in range(2)]
    trail = front.shape[0] - PIV * NBL
    dma = pltpu.SemaphoreType.DMA
    outs = [
        (trail, BLK),
        grid_of + (CAP * BLK, BLK),
        (4, 4) + panel.shape,
    ] + [grid_of + (rows, BLK) for rows in sizes]
    small = pltpu.VMEM(grid_of + (CAP, BLK), jnp.int32)
    return pl.pallas_call(
        front_kernel,
        out_shape=[jax.ShapeDtypeStruct(shape, jnp.bfloat16) for shape in outs],
        in_specs=[smem, smem, smem, any_space, any_space, any_space, any_space, any_space],
        out_specs=[any_space] * len(outs),
        scratch_shapes=[
            pltpu.VMEM(grid_of + (CAP * BLK, BLK), jnp.bfloat16),
            pltpu.VMEM(blocks.shape, jnp.bfloat16),
            pltpu.VMEM((128 * CAP, BLK, BLK), jnp.float32),
            pltpu.VMEM((trail, BLK), jnp.bfloat16),
            pltpu.VMEM((PIV * NBL, BLK), jnp.bfloat16),
            pltpu.VMEM(pivot.shape, jnp.bfloat16),
            pltpu.VMEM((PIV, NBL * BLK), jnp.bfloat16),
            pltpu.VMEM((PIV, NBL * BLK), jnp.bfloat16),
            pltpu.VMEM((2, 256, PIV), jnp.bfloat16),
            pltpu.VMEM((256, NBL * BLK), jnp.float32),
            pltpu.VMEM((2, 256 * NBL, BLK), jnp.bfloat16),
            pltpu.VMEM((BLK * NBL, BLK), jnp.float32),
            small, small, small,
            pltpu.VMEM((128 * CAP, BLK), jnp.int32),
            pltpu.VMEM((8, BLK), jnp.int32),
            pltpu.SMEM((8, BLK), jnp.int32),
            dma((4, 3)), dma((4, 3)), dma((4, 3)),
            dma((40,)), dma((40,)), dma,
            dma((4,)), dma, dma, dma((2,)), dma((2,)),
        ],
        compiler_params=pltpu.CompilerParams(
            collective_id=0, has_side_effects=True, vmem_limit_bytes=58 * 2**20
        ),
        name="front",
    )(table, size, pattern, blocks, meta, front, pivot, panel)[0]


def per_device(
    front_entries,
    contributions,
    dest_owner,
    dest_row,
    dest_col,
    pivot_inverse,
    panel,
    pattern,
    front_size,
):
    devices = lax.axis_size("front") * lax.axis_size("grid")
    count = contributions.shape[0]
    total_rows = front_entries.shape[1]
    sentinel = total_rows // BLK * NBL
    owner = dest_owner[:, 0]
    position = jnp.arange(count, dtype=jnp.int32)
    same_owner = owner[:, None] == owner[None, :]
    before = position[None, :] < position[:, None]
    ranking = jnp.sum((same_owner & before).astype(jnp.int32), axis=1)
    slots = owner * CAP + ranking
    table = jnp.zeros((devices * CAP,), jnp.int32).at[slots].set(position)
    targets = (
        jnp.full((devices * CAP,), sentinel, jnp.int32).at[slots].set(dest_row * NBL + dest_col)
    )
    meta = jnp.broadcast_to(targets.reshape(8, 4, 4, CAP, 1), (8, 4, 4, CAP, BLK))
    out = schur_of_front(
        table,
        front_size,
        pattern[0, :, :, 0],
        contributions,
        meta,
        front_entries.reshape(total_rows * NBL, BLK),
        pivot_inverse[0],
        panel[0],
    )
    return out.reshape(1, -1, NBL, BLK)


def solution(mesh):
    placed = (
        P("front", None, None, "grid"),
        P(("front", "grid"), None, None),
        P(("front", "grid"), None),
        P(("front", "grid")),
        P(("front", "grid")),
        P("front", None, None),
        P("front", "grid", None),
        P("front", None, None, "grid"),
        P("front"),
    )
    return jax.shard_map(
        per_device,
        mesh=mesh,
        in_specs=placed,
        out_specs=P("front", None, None, "grid"),
        check_vma=False,
    )
```

time: 383 us -> 238 us (0.62); the launches traced: 377 us -> 237 us
  Pallas kernels: 0 us -> 221 us
  local copies, waits for them, and re-layouts: 129 us -> 13.2 us
  waiting for transfers between devices: 95.7 us -> 0 us
  other arithmetic: 97.9 us -> 2.33 us
  starting transfers between devices: 21.7 us -> 0 us
  matrix products: 18.1 us -> 0 us
  between operations: 14.2 us -> 0.69 us
    pallas_call x0 -> x1, Pallas kernels: none -> 221 us  [schur_of_front(): pl.pallas_call(front_kernel, out_shape=[jax.ShapeDtypeStruct(shape, jnp.b...]
    all_to_all x2 -> x0, waiting for transfers between devices: 95 us -> none  [the longest x1 95 us: per_device(): lax.all_to_all(outgoing.reshape(devices, CAP, BLK, BLK), ('front', 'grid'...]
    convert_element_type x2 -> x0, local copies, waits for them, and re-layouts: 52.5 us -> none  [the longest x1 39.9 us: per_device(): return result.astype(jnp.bfloat16).reshape(1, trail, NBL, BLK)]
    scatter-add x1 -> x0, other arithmetic: 51.6 us -> none  [per_device(): store.at[block_row, :, block_col, :]]
    convert_element_type x4 -> x0, other arithmetic: 31.8 us -> none  [the longest x1 13 us: per_device(): return result.astype(jnp.bfloat16).reshape(1, trail, NBL, BLK)]
    reshape x3 -> x0, local copies, waits for them, and re-layouts: 29.3 us -> none  [the longest x1 17.4 us: per_device(): update = update.reshape(trail_blocks, BLK, NBL, BLK)]
    scatter x1, local copies, waits for them, and re-layouts: 24.1 us -> 1.67 us  [per_device(): table = jnp.zeros((devices * CAP,), jnp.int32).at[slots].set(position)]
    all_to_all x2 -> x0, starting transfers between devices: 21.7 us -> none  [the longest x1 11.5 us: per_device(): lax.all_to_all(targets.reshape(devices, CAP), ('front', 'grid'), split_ax...]
  transfers between devices with their start and end apart: 3 -> 0, of which waited for: 1 -> 0; matrix products, arithmetic and copies ran while one was open for 40% -> 0% of each run, Pallas kernels for 0% -> 0%
where the time goes in v2:
time: 238 us; the launch traced here: 237 us
  Pallas kernels  221 us (93%)
  local copies, waits for them, and re-layouts  13.2 us (6%)
    pallas_call x1, Pallas kernels, schur_of_front(): pl.pallas_call(front_kernel, out_shape=[jax.ShapeDtypeStruct(shape, jnp.b...  221 us
    unnamed x2, local copies, waits for them, and re-layouts  9.43 us

profile of v2, /device:TPU:1, one launch (start us, length us, event | category | flops | bytes accessed | tf_op | source)
XLA Modules:
  0.0 236.8 jit_solution(11093404069725256796)
XLA Ops:
  0.7 0.7 multiply_add_fusion
  1.4 0.9 convert_reduce_fusion
  2.3 0.7 compare_select_fusion
  3.0 1.1 scatter_custom_fusion.1
  4.1 1.7 scatter_custom_fusion.table
  5.8 1.4 copy.12
  7.1 0.2 broadcast_in_dim.19
  7.3 0.9 broadcast_in_dim.20.meta
  8.2 220.6 %front.1 = (bf16[32768,128]{1,0:T(8,128)(2,1)}, bf16[8,4,4,256,128]{4,3,2,1,0:T(8,128)(2,1)}, bf16[4,4,512,1024]{3,2,1,0:T(8,128)(2,1)}, bf16[8,4,4,96,128]{4,3,...) custom-call(s32[256]{0:T(256)} %scatter_custom_fusion.table, ...), custom_call_target="tpu_custom_call" | custom-call | tf_op jit(solution)/shard_map/front/pallas_call | solution.py:390
  228.8 8.1 %copy.15 = bf16[1,8192,4,128]{3,2,1,0:T(4,128)(2,1)} copy(bf16[1,8192,4,128]{3,2,1,0:T(4,128)(2,1)} %bitcast.11) | data formatting | bytes 16777216
  (1 shorter events, 0.0 us)

commit v3 on v2

v3 whole, which is shorter than its diff:
```python
import functools

import jax
import jax.numpy as jnp
from jax import lax
from jax.experimental import pallas as pl
from jax.experimental.pallas import tpu as pltpu
from jax.sharding import PartitionSpec as P

BLK = 128
PIV = 1024
NBL = 4
CAP = 2
MESH = pl.DeviceIdType.MESH
PARTS = ((0, 96), (96, 80), (176, 80))
DEPTH = 4
ORDERS = ((0, 1, 2), (1, 2, 0), (2, 0, 1))


def at_axis(axis, where, rows=None):
    index = [slice(None)] * 5
    index[axis] = where
    if rows is not None:
        index[3] = pl.ds(rows[0], rows[1])
    return tuple(index)


def front_kernel(
    size, pattern, owner, spots, blocks, front, pivot, panel,
    out, arrived, panel_full,
    slots, stage1, stage2, blocks_v, sums, pivot_v, top, factor, panel_v,
    update0, update1, wide0, wide1,
    m0, m1, m2, m3, places, chain_v, chain,
    send_sem, recv_sem, own_sem, gsend_sem, grecv_sem,
    load_sem, lower_sem, arrived_sem, chain_sem, panel_sem, out_sem,
):
    f = lax.axis_index("front")
    g = lax.axis_index("grid")
    y, z = g // 4, g % 4
    me = (f, y, z)

    def device(axis, coordinate):
        if axis == 0:
            return (coordinate, g)
        if axis == 1:
            return (f, coordinate * 4 + z)
        return (f, y * 4 + coordinate)

    def peer(axis, d):
        if axis == 0:
            return ((f // 2 + d // 2) % 4) * 2 + (f + d) % 2
        return (me[axis] + d) % 4

    offsets = ((2, 6, 4, 3, 7, 5, 1), (1, 3, 2), (1, 3, 2))

    barrier = pltpu.get_barrier_semaphore()
    for axis in range(3):
        for d in offsets[axis]:
            pl.semaphore_signal(
                barrier, inc=1, device_id=device(axis, peer(axis, d)), device_id_type=MESH
            )

    load_blocks = pltpu.make_async_copy(blocks, blocks_v, load_sem.at[0])
    load_top = pltpu.make_async_copy(front.at[0], stage1.at[0], load_sem.at[1])
    load_pivot = pltpu.make_async_copy(pivot, pivot_v, load_sem.at[2])
    load_lower = [
        pltpu.make_async_copy(front.at[1 + i], slots.at[i], lower_sem.at[i]) for i in range(8)
    ]
    load_blocks.start()

    def make_slots():
        shape = (128, owner.shape[1])
        whose = lax.broadcasted_iota(jnp.int32, shape, 0)
        block = lax.broadcasted_iota(jnp.int32, shape, 1)
        spot = jnp.broadcast_to(spots[...], shape)
        match = jnp.broadcast_to(owner[...], shape) == whose
        first = jnp.min(jnp.where(match, block, shape[1]), axis=1, keepdims=True)
        second = jnp.max(jnp.where(match, block, -1), axis=1, keepdims=True)
        nowhere = front.shape[0] * 16 * CAP
        square = (128, BLK)
        for j, (chosen, there) in enumerate(
            ((first, second >= 0), (second, second > first))
        ):
            hit = jnp.max(jnp.where(block == chosen, spot, 0), axis=1, keepdims=True)
            hit = jnp.where(there, hit, nowhere)
            places[pl.ds(j, 128, stride=CAP), :] = jnp.broadcast_to(hit, square)
            index = jnp.broadcast_to(jnp.where(there, chosen, 0), square)
            diagonal = lax.broadcasted_iota(jnp.int32, square, 0) == lax.broadcasted_iota(
                jnp.int32, square, 1
            )
            chain_v[j : j + 1, :] = jnp.sum(
                jnp.where(diagonal, index, 0), axis=0, keepdims=True
            )
        copy = pltpu.make_async_copy(chain_v, chain, chain_sem)
        copy.start()

        def spread(d, carry):
            m0[d // 16, (d // 4) % 4, d % 4] = places[pl.ds(d * CAP, CAP), :]
            return carry

        lax.fori_loop(0, 128, spread, 0)
        copy.wait()

    def fill(d, carry):
        for j in range(CAP):
            slots[d // 16, (d // 4) % 4, d % 4, pl.ds(j * BLK, BLK), :] = blocks_v[chain[j, d]]
        return carry

    chains = []
    for part, (rows, order) in enumerate(zip(PARTS, ORDERS)):
        chains.append(((slots, rows), (stage1, rows), (stage2, rows), (arrived, rows), order))
    chains.append(((m0, None), (m1, None), (m2, None), (m3, None), (0, 1, 2)))

    def view(buffer, axis, where):
        ref, rows = buffer
        return ref.at[at_axis(axis, where, rows)]

    pending = {}

    def start(part, stage):
        steps = chains[part]
        source, target, axis = steps[stage], steps[stage + 1], steps[4][stage]
        own = pltpu.make_async_copy(
            view(source, axis, me[axis]), view(target, axis, me[axis]), own_sem.at[part, stage]
        )
        own.start()
        for d in offsets[axis]:
            there = peer(axis, d)
            pltpu.make_async_remote_copy(
                src_ref=view(source, axis, there),
                dst_ref=view(target, axis, me[axis]),
                send_sem=send_sem.at[part, stage],
                recv_sem=recv_sem.at[part, stage],
                device_id=device(axis, there),
                device_id_type=MESH,
            ).start()
        count = len(offsets[axis])
        whole = pltpu.make_async_remote_copy(
            src_ref=view(source, axis, pl.ds(0, count)),
            dst_ref=view(target, axis, pl.ds(0, count)),
            send_sem=send_sem.at[part, stage],
            recv_sem=recv_sem.at[part, stage],
            device_id=device(axis, peer(axis, 1)),
            device_id_type=MESH,
        )
        pending[part, stage] = (own, whole)

    def finish(part, stage):
        own, whole = pending[part, stage]
        own.wait()
        whole.wait_recv()

    gathers = []
    got = {}

    def place(half, dp, ds):
        if half == 0:
            return (y + dp + 4) % 4, (z + ds + 4) % 4
        return (y + ds + 4) % 4, (z + dp + 4) % 4

    def give(key, half, dp, ds, piece, along, step):
        py, pz = place(half, dp, ds)
        first, count = half * 256, 256
        if piece is not None:
            first, count = first + 128 * piece, 128
        rows = pl.ds(first, count)
        axis = (1, 2)[half] if along == 0 else (2, 1)[half]
        source = panel.at[rows] if (dp, ds) == (0, 0) else panel_full.at[py, pz, rows]
        index = len(gathers)
        copy = pltpu.make_async_remote_copy(
            src_ref=source,
            dst_ref=panel_full.at[py, pz, rows],
            send_sem=gsend_sem.at[index],
            recv_sem=grecv_sem.at[index],
            device_id=device(axis, peer(axis, step % 4)),
            device_id_type=MESH,
        )
        copy.start()
        gathers.append(copy)
        got[key] = copy

    def each(act):
        for half in (0, 1):
            for step, piece in ((1, 0), (-1, 1)):
                act(half, step, piece)

    def first_line():
        each(lambda h, s, p: give((h, "p", s), h, 0, 0, None, 0, s))

    def second_line(dp):
        each(lambda h, s, p: give((h, "s", dp, s), h, dp, 0, None, 1, s))

    def first_forward():
        each(lambda h, s, p: got[h, "p", s].wait_recv())
        each(lambda h, s, p: give((h, "pf", s), h, -s, 0, p, 0, s))

    def second_forward(dp):
        each(lambda h, s, p: got[h, "s", dp, s].wait_recv())
        each(lambda h, s, p: give((h, "sf", dp, s), h, dp, -s, p, 1, s))

    def landed(kind, *rest):
        each(lambda h, s, p: got[(h, kind) + rest + (s,)].wait_recv())

    def make_tables():
        def spread(d, carry):
            places[pl.ds(d * CAP, CAP), :] = m3[d // 16, (d // 4) % 4, d % 4]
            return carry

        lax.fori_loop(0, 128, spread, 0)
        where = places[...]
        slot = lax.broadcasted_iota(jnp.int32, where.shape, 0)
        lane = lax.broadcasted_iota(jnp.int32, where.shape, 1)

        def latest(same):
            found = jnp.max(jnp.where(same, slot, -1), axis=0, keepdims=True)
            return jnp.where(found < 0, CAP * 128, found)

        for half in range(2):
            mine = lane + half * BLK
            along = jnp.sum(jnp.where(slot == mine, where, 0), axis=0, keepdims=True)
            same = jnp.logical_and(where == along, slot < mine)
            chain_v[half : half + 1, :] = latest(same)
        for third in range(3):
            same = where == lane + third * BLK
            chain_v[2 + third : 3 + third, :] = latest(same)
        copy = pltpu.make_async_copy(chain_v, chain, chain_sem)
        copy.start()
        copy.wait()

    def block_of(t):
        d = t // CAP
        return slots[d // 16, (d // 4) % 4, d % 4, pl.ds((t % CAP) * BLK, BLK), :].astype(
            jnp.float32
        )

    count = sums.shape[0] - 1

    def add_up(arrivals):
        sums[count] = jnp.zeros((BLK, BLK), jnp.float32)

        def one(t, carry):
            sums[t] = block_of(t) + sums[chain[t // BLK, t % BLK]]
            return carry

        each_time = count // len(arrivals)
        for i, copy in enumerate(arrivals):
            copy.wait()
            lax.fori_loop(i * each_time, (i + 1) * each_time, one, 0)

    def assembled(source, row):
        d = 2 * row % 16
        for i, wide in enumerate((wide0, wide1)):
            wide[pl.ds(0, 256), :] = source[d // 4, d % 4 + i].astype(jnp.float32)
        values = []
        for k in range(NBL):
            p = row * NBL + k
            total = sums[chain[2 + p // BLK, p % BLK]]
            part = pl.ds(k, BLK // 2, stride=NBL)
            value = jnp.concatenate([wide0[part, :], wide1[part, :]], axis=0)
            values.append((value + total).astype(jnp.bfloat16))
        return d, values

    def make_factor():
        def one(row, carry):
            _, values = assembled(stage1.at[0], row)
            for k in range(NBL):
                top[pl.ds(row * BLK, BLK), pl.ds(k * BLK, BLK)] = values[k]
            return carry

        lax.fori_loop(0, PIV // BLK, one, 0)
        load_pivot.wait()
        factor[...] = jnp.dot(
            pivot_v[...], top[...], preferred_element_type=jnp.float32
        ).astype(jnp.bfloat16)

    def make_lower():
        for i in range(8):
            load_lower[i].wait()

            def one(j, carry):
                d, values = assembled(slots.at[i], PIV // BLK + i * 8 + j)
                for k in range(NBL):
                    slots[i, d // 4, d % 4 + k // 2, pl.ds(k % 2 * BLK, BLK), :] = values[k]
                return carry

            lax.fori_loop(0, 8, one, 0)

    limit = size[0]

    def load(i, half, decode):
        rows = pl.ds(half * 256, 256)
        if decode is None:
            source = panel.at[rows]
        else:
            py, pz = decode(i, half)
            source = panel_full.at[py, pz, rows]
        return pltpu.make_async_copy(
            source, panel_v.at[i % DEPTH, half], panel_sem.at[i % DEPTH, half]
        )

    def prefetch(first, count, decode):
        for i in range(min(DEPTH, count)):
            for half in (0, 1):
                load(first + i, half, None if first + i == 0 else decode).start()

    def updates(first, count, decode):
        def one(i, carry):
            for half, update in ((0, update0), (1, update1)):
                load(i, half, decode).wait()
                update[...] = jnp.dot(
                    panel_v[i % DEPTH, half], factor[...], preferred_element_type=jnp.float32
                )
            for half, update in ((0, update0), (1, update1)):
                py, pz = decode(i, half)
                for j, wide in ((0, wide0), (1, wide1)):
                    row = (py * 4 + pz) * 4 + half * 2 + j
                    d = 2 * row
                    for k in range(NBL):
                        keep = jnp.logical_and(row < limit, k * 16 + g < limit)
                        chosen = pattern[k, 0, row].astype(jnp.float32)
                        lower = slots[
                            d // 16, (d // 4) % 4, d % 4 + k // 2, pl.ds(k % 2 * BLK, BLK), :
                        ].astype(jnp.float32)
                        taken = update[pl.ds(j * BLK, BLK), pl.ds(k * BLK, BLK)]
                        wide[pl.ds(k, BLK, stride=NBL), :] = jnp.where(
                            keep, lower - chosen * taken, 0.0
                        )
                    for part in range(2):
                        stage2[i // 2, i % 2 * 2 + half, 2 * j + part] = wide[
                            pl.ds(part * 256, 256), :
                        ].astype(jnp.bfloat16)
                pltpu.make_async_copy(
                    stage2.at[i // 2, i % 2 * 2 + half],
                    out.at[pl.ds((py * 4 + pz) * 8 + half * 4, 4)],
                    out_sem,
                ).start()

            if count > DEPTH:

                @pl.when(i + DEPTH < first + count)
                def _():
                    for half in (0, 1):
                        load(i + DEPTH, half, decode).start()

            return carry

        lax.fori_loop(first, first + count, one, 0)

    def spot(half, dp, ds):
        return (y + dp * (1 - half) + ds * half) % 4, (z + dp * half + ds * (1 - half)) % 4

    def near(i, half):
        a, b = i % 3, i // 3
        return spot(half, a + a // 2, b + b // 2)

    def far(i, half):
        a, b = (i - 9) % 3, (i - 9) // 3
        d = a + a // 2
        return spot(half, d * (1 - b) + 2 * b, d * b + 2 * (1 - b))

    def last(i, half):
        return spot(half, 2, 2)

    pl.semaphore_wait(barrier, 13)
    first_line()
    second_line(0)
    load_pivot.start()
    make_slots()
    start(3, 0)
    load_blocks.wait()
    lax.fori_loop(0, 128, fill, 0)
    for part in range(3):
        start(part, 0)
    finish(3, 0)
    start(3, 1)
    for part in range(3):
        finish(part, 0)
        start(part, 1)
    finish(3, 1)
    start(3, 2)
    first_forward()
    second_forward(0)
    for part in range(3):
        finish(part, 1)
        start(part, 2)
    second_line(-1)
    finish(3, 2)
    make_tables()
    for part in range(3):
        pending[part, 0][1].wait_send()
        pending[part, 1][1].wait_send()
    load_top.start()
    for part in range(3):
        finish(part, 2)
    back = [
        pltpu.make_async_copy(arrived.at[i], slots.at[i], arrived_sem.at[i]) for i in range(8)
    ]
    for copy in back:
        copy.start()
    second_line(1)
    landed("pf")
    second_line(2)
    second_forward(-1)
    add_up(back)
    for copy in load_lower:
        copy.start()
    second_forward(1)
    prefetch(0, 9, near)
    load_top.wait()
    make_factor()
    make_lower()
    second_forward(2)
    for part in range(3):
        pending[part, 2][1].wait_send()
    updates(0, 9, near)
    for dp in (0, -1, 1):
        landed("sf", dp)
    prefetch(9, 6, far)
    updates(9, 6, far)
    landed("sf", 2)
    prefetch(15, 1, last)
    updates(15, 1, last)
    pltpu.make_async_copy(stage2, arrived, out_sem).wait()
    for (part, stage), (_, whole) in pending.items():
        if part == 3:
            whole.wait_send()
    for copy in gathers:
        copy.wait_send()


def schur_of_front(size, pattern, owner, spots, blocks, front, pivot, panel):
    grid_of = (8, 4, 4)
    any_space = pl.BlockSpec(memory_space=pl.ANY)
    smem = pl.BlockSpec(memory_space=pltpu.SMEM)
    vmem = pl.BlockSpec(memory_space=pltpu.VMEM)
    dma = pltpu.SemaphoreType.DMA
    outs = [
        (128, CAP * BLK, BLK),
        grid_of + (CAP * BLK, BLK),
        (4, 4) + panel.shape,
    ]
    small = pltpu.VMEM(grid_of + (CAP, BLK), jnp.int32)
    large = pltpu.VMEM(grid_of + (CAP * BLK, BLK), jnp.bfloat16)
    return pl.pallas_call(
        front_kernel,
        out_shape=[jax.ShapeDtypeStruct(shape, jnp.bfloat16) for shape in outs],
        in_specs=[smem, smem, vmem, vmem, any_space, any_space, any_space, any_space],
        out_specs=[any_space] * len(outs),
        scratch_shapes=[
            large, large, large,
            pltpu.VMEM(blocks.shape, jnp.bfloat16),
            pltpu.VMEM((128 * CAP + 1, BLK, BLK), jnp.float32),
            pltpu.VMEM(pivot.shape, jnp.bfloat16),
            pltpu.VMEM((PIV, NBL * BLK), jnp.bfloat16),
            pltpu.VMEM((PIV, NBL * BLK), jnp.bfloat16),
            pltpu.VMEM((DEPTH, 2, 256, PIV), jnp.bfloat16),
            pltpu.VMEM((256, NBL * BLK), jnp.float32),
            pltpu.VMEM((256, NBL * BLK), jnp.float32),
            pltpu.VMEM((BLK * NBL, BLK), jnp.float32),
            pltpu.VMEM((BLK * NBL, BLK), jnp.float32),
            small, small, small, small,
            pltpu.VMEM((128 * CAP, BLK), jnp.int32),
            pltpu.VMEM((8, BLK), jnp.int32),
            pltpu.SMEM((8, BLK), jnp.int32),
            dma((4, 3)), dma((4, 3)), dma((4, 3)),
            dma((40,)), dma((40,)),
            dma((3,)), dma((8,)), dma((8,)), dma, dma((DEPTH, 2)), dma,
        ],
        compiler_params=pltpu.CompilerParams(
            collective_id=0, has_side_effects=True, vmem_limit_bytes=62 * 2**20
        ),
        name="front",
    )(size, pattern, owner, spots, blocks, front, pivot, panel)[0]


PIECES = 8


def pass_kernel(source, target, held, in_sem, out_sem):
    rows = source.shape[0] // PIECES
    steps = []
    for i in range(PIECES):
        part = pl.ds(i * rows, rows)
        steps.append(
            (
                pltpu.make_async_copy(source.at[part], held.at[part], in_sem.at[i]),
                pltpu.make_async_copy(held.at[part], target.at[part], out_sem.at[i]),
            )
        )
    for take, _ in steps:
        take.start()
    for take, give in steps:
        take.wait()
        give.start()
    for _, give in steps:
        give.wait()


def pass_on(array):
    any_space = pl.BlockSpec(memory_space=pl.ANY)
    return pl.pallas_call(
        pass_kernel,
        out_shape=jax.ShapeDtypeStruct(array.shape, array.dtype),
        in_specs=[any_space],
        out_specs=any_space,
        scratch_shapes=[
            pltpu.VMEM(array.shape, array.dtype),
            pltpu.SemaphoreType.DMA((PIECES,)),
            pltpu.SemaphoreType.DMA((PIECES,)),
        ],
        compiler_params=pltpu.CompilerParams(vmem_limit_bytes=60 * 2**20),
        name="pass_on",
    )(array)


def per_device(
    front_entries,
    contributions,
    dest_owner,
    dest_row,
    dest_col,
    pivot_inverse,
    panel,
    pattern,
    front_size,
):
    out = schur_of_front(
        front_size,
        pattern[0, :, :, 0].T.reshape(NBL, 1, -1),
        dest_owner.reshape(1, -1),
        (dest_row * NBL + dest_col).reshape(1, -1),
        contributions,
        front_entries.reshape(-1, 4, 4, CAP * BLK, BLK),
        pivot_inverse[0],
        panel[0],
    )
    out = pass_on(out)
    return out.reshape(1, -1, NBL, BLK)


def solution(mesh):
    placed = (
        P("front", None, None, "grid"),
        P(("front", "grid"), None, None),
        P(("front", "grid"), None),
        P(("front", "grid")),
        P(("front", "grid")),
        P("front", None, None),
        P("front", "grid", None),
        P("front", None, None, "grid"),
        P("front"),
    )
    return jax.shard_map(
        per_device,
        mesh=mesh,
        in_specs=placed,
        out_specs=P("front", None, None, "grid"),
        check_vma=False,
    )
```

time: 238 us -> 204 us (0.86)
  Pallas kernels: 221 us -> 200 us
  local copies, waits for them, and re-layouts: 13.2 us -> 0 us
    pallas_call x1, Pallas kernels: 221 us -> 194 us  [schur_of_front(): pl.pallas_call(front_kernel, out_shape=[jax.ShapeDtypeStruct(shape, jnp.b...]
    unnamed x2 -> x0, local copies, waits for them, and re-layouts: 9.43 us -> none
    pallas_call x0 -> x1, Pallas kernels: none -> 6.42 us  [pass_on(): pl.pallas_call(pass_kernel, out_shape=jax.ShapeDtypeStruct(array.shape, a...]
    scatter x2 -> x0, local copies, waits for them, and re-layouts: 2.76 us -> none  [the longest x1 1.67 us: per_device(): table = jnp.zeros((devices * CAP,), jnp.int32).at[slots].set(position)]
where the time goes in v3:
time: 204 us; the launch traced here: 202 us
  Pallas kernels  200 us (98%)
    pallas_call x1, Pallas kernels, schur_of_front(): pl.pallas_call(front_kernel, out_shape=[jax.ShapeDtypeStruct(shape, jnp.b...  194 us
    pallas_call x1, Pallas kernels, pass_on(): pl.pallas_call(pass_kernel, out_shape=jax.ShapeDtypeStruct(array.shape, a...  6.42 us

profile of v3, /device:TPU:1, one launch (start us, length us, event | category | flops | bytes accessed | tf_op | source)
XLA Modules:
  0.0 202.1 jit_solution(8948473477487027196)
XLA Ops:
  0.7 1.3 multiply_add_fusion
  1.9 193.7 %front.1 = (bf16[128,256,128]{2,1,0:T(8,128)(2,1)}, bf16[8,4,4,256,128]{4,3,2,1,0:T(8,128)(2,1)}, bf16[4,4,512,1024]{3,2,1,0:T(8,128)(2,1)}) custom-call(s32[1]{0:T(128)S(6)} %copy.10.size, s32[4,1,64]{2,1,0:T(1,128)} %bitcast.15, s32[1,160]{1,0:T(1,128)} %bitcast.16, s32[1,160]{1,0:T(1,128)} %bitcast.14, bf16[160,128,128]{2,1,0:T(8,128)(2,1)} %blocks.1, ...), custom_call_target="tpu_custom_call" | custom-call | tf_op jit(solution)/shard_map/front/pallas_call | solution.py:444
  195.6 6.4 %pass_on.1 = bf16[128,256,128]{2,1,0:T(8,128)(2,1)} custom-call(bf16[128,256,128]{2,1,0:T(8,128)(2,1)} %get-tuple-element.6.source), custom_call_target="tpu_custom_call" | custom-call | tf_op jit(solution)/shard_map/pass_on/pallas_call | solution.py:501

commit v4 on v3

--- a/solution.py
+++ b/solution.py
@@ -25,14 +25,27 @@
     return tuple(index)
 
 
+def schur_rows(update, wides, lower, write, pattern, limit, column, first):
+    for j, wide in enumerate(wides):
+        row = first + j
+        for k in range(NBL):
+            keep = jnp.logical_and(row < limit, k * 16 + column < limit)
+            chosen = pattern[k, 0, row].astype(jnp.float32)
+            taken = update[pl.ds(j * BLK, BLK), pl.ds(k * BLK, BLK)]
+            here = lower(row, k).astype(jnp.float32)
+            wide[pl.ds(k, BLK, stride=NBL), :] = jnp.where(keep, here - chosen * taken, 0.0)
+        for part in range(2):
+            write(row * 2 + part, wide[pl.ds(part * 256, 256), :].astype(jnp.bfloat16))
+
+
 def front_kernel(
-    size, pattern, owner, spots, blocks, front, pivot, panel,
-    out, arrived, panel_full,
-    slots, stage1, stage2, blocks_v, sums, pivot_v, top, factor, panel_v,
+    size, pattern, owner, rows_to, cols_to, blocks, front, pivot, panel,
+    out, arrived, panel_full, factor,
+    slots, stage1, blocks_v, sums, pivot_v, top, panel_v,
     update0, update1, wide0, wide1,
     m0, m1, m2, m3, places, chain_v, chain,
     send_sem, recv_sem, own_sem, gsend_sem, grecv_sem,
-    load_sem, lower_sem, arrived_sem, chain_sem, panel_sem, out_sem,
+    load_sem, lower_sem, arrived_sem, chain_sem, panel_sem, leave_sem,
 ):
     f = lax.axis_index("front")
     g = lax.axis_index("grid")
@@ -72,7 +85,7 @@
         shape = (128, owner.shape[1])
         whose = lax.broadcasted_iota(jnp.int32, shape, 0)
         block = lax.broadcasted_iota(jnp.int32, shape, 1)
-        spot = jnp.broadcast_to(spots[...], shape)
+        spot = jnp.broadcast_to(rows_to[...] * NBL + cols_to[...], shape)
         match = jnp.broadcast_to(owner[...], shape) == whose
         first = jnp.min(jnp.where(match, block, shape[1]), axis=1, keepdims=True)
         second = jnp.max(jnp.where(match, block, -1), axis=1, keepdims=True)
@@ -108,7 +121,7 @@
 
     chains = []
     for part, (rows, order) in enumerate(zip(PARTS, ORDERS)):
-        chains.append(((slots, rows), (stage1, rows), (stage2, rows), (arrived, rows), order))
+        chains.append(((slots, rows), (stage1, rows), (out, rows), (arrived, rows), order))
     chains.append(((m0, None), (m1, None), (m2, None), (m3, None), (0, 1, 2)))
 
     def view(buffer, axis, where):
@@ -304,6 +317,13 @@
                 load(first + i, half, None if first + i == 0 else decode).start()
 
     def updates(first, count, decode):
+        def lower(row, k):
+            d = 2 * row
+            return slots[d // 16, (d // 4) % 4, d % 4 + k // 2, pl.ds(k % 2 * BLK, BLK), :]
+
+        def write(d, value):
+            out[d // 16, (d // 4) % 4, d % 4] = value
+
         def one(i, carry):
             for half, update in ((0, update0), (1, update1)):
                 load(i, half, decode).wait()
@@ -312,28 +332,8 @@
                 )
             for half, update in ((0, update0), (1, update1)):
                 py, pz = decode(i, half)
-                for j, wide in ((0, wide0), (1, wide1)):
-                    row = (py * 4 + pz) * 4 + half * 2 + j
-                    d = 2 * row
-                    for k in range(NBL):
-                        keep = jnp.logical_and(row < limit, k * 16 + g < limit)
-                        chosen = pattern[k, 0, row].astype(jnp.float32)
-                        lower = slots[
-                            d // 16, (d // 4) % 4, d % 4 + k // 2, pl.ds(k % 2 * BLK, BLK), :
-                        ].astype(jnp.float32)
-                        taken = update[pl.ds(j * BLK, BLK), pl.ds(k * BLK, BLK)]
-                        wide[pl.ds(k, BLK, stride=NBL), :] = jnp.where(
-                            keep, lower - chosen * taken, 0.0
-                        )
-                    for part in range(2):
-                        stage2[i // 2, i % 2 * 2 + half, 2 * j + part] = wide[
-                            pl.ds(part * 256, 256), :
-                        ].astype(jnp.bfloat16)
-                pltpu.make_async_copy(
-                    stage2.at[i // 2, i % 2 * 2 + half],
-                    out.at[pl.ds((py * 4 + pz) * 8 + half * 4, 4)],
-                    out_sem,
-                ).start()
+                first_row = (py * 4 + pz) * 4 + half * 2
+                schur_rows(update, (wide0, wide1), lower, write, pattern, limit, g, first_row)
 
             if count > DEPTH:
 
@@ -353,13 +353,11 @@
         a, b = i % 3, i // 3
         return spot(half, a + a // 2, b + b // 2)
 
-    def far(i, half):
-        a, b = (i - 9) % 3, (i - 9) // 3
-        d = a + a // 2
-        return spot(half, d * (1 - b) + 2 * b, d * b + 2 * (1 - b))
-
-    def last(i, half):
-        return spot(half, 2, 2)
+    def middle(i, half):
+        return spot(half, 2 * (1 - (i - 9) // 3), (i - 6) % 4)
+
+    def late(i, half):
+        return spot(half, 3 - 2 * (i - 13), 2)
 
     pl.semaphore_wait(barrier, 13)
     first_line()
@@ -409,18 +407,26 @@
     load_top.wait()
     make_factor()
     make_lower()
-    second_forward(2)
     for part in range(3):
         pending[part, 2][1].wait_send()
+    final = (y + 2) % 4 * 4 + (z + 2) % 4
+    leave_rows = pltpu.make_async_copy(
+        slots.at[final // 2, pl.ds(final % 2 * 2, 2)],
+        out.at[final // 2, pl.ds(final % 2 * 2, 2)],
+        leave_sem,
+    )
+    leave_rows.start()
     updates(0, 9, near)
-    for dp in (0, -1, 1):
+    second_forward(2)
+    landed("sf", 0)
+    prefetch(9, 4, middle)
+    updates(9, 4, middle)
+    for i, dp in ((13, -1), (14, 1)):
         landed("sf", dp)
-    prefetch(9, 6, far)
-    updates(9, 6, far)
+        prefetch(i, 1, late)
+        updates(i, 1, late)
+    leave_rows.wait()
     landed("sf", 2)
-    prefetch(15, 1, last)
-    updates(15, 1, last)
-    pltpu.make_async_copy(stage2, arrived, out_sem).wait()
     for (part, stage), (_, whole) in pending.items():
         if part == 3:
             whole.wait_send()
@@ -428,30 +434,30 @@
         copy.wait_send()
 
 
-def schur_of_front(size, pattern, owner, spots, blocks, front, pivot, panel):
+def front_parts(size, pattern, owner, rows_to, cols_to, blocks, front, pivot, panel):
     grid_of = (8, 4, 4)
     any_space = pl.BlockSpec(memory_space=pl.ANY)
     smem = pl.BlockSpec(memory_space=pltpu.SMEM)
     vmem = pl.BlockSpec(memory_space=pltpu.VMEM)
     dma = pltpu.SemaphoreType.DMA
     outs = [
-        (128, CAP * BLK, BLK),
-        grid_of + (CAP * BLK, BLK),
-        (4, 4) + panel.shape,
+        pltpu.VMEM(grid_of + (CAP * BLK, BLK), jnp.bfloat16),
+        jax.ShapeDtypeStruct(grid_of + (CAP * BLK, BLK), jnp.bfloat16),
+        jax.ShapeDtypeStruct((4, 4) + panel.shape, jnp.bfloat16),
+        pltpu.VMEM((PIV, NBL * BLK), jnp.bfloat16),
     ]
     small = pltpu.VMEM(grid_of + (CAP, BLK), jnp.int32)
     large = pltpu.VMEM(grid_of + (CAP * BLK, BLK), jnp.bfloat16)
     return pl.pallas_call(
         front_kernel,
-        out_shape=[jax.ShapeDtypeStruct(shape, jnp.bfloat16) for shape in outs],
-        in_specs=[smem, smem, vmem, vmem, any_space, any_space, any_space, any_space],
-        out_specs=[any_space] * len(outs),
+        out_shape=outs,
+        in_specs=[smem, smem, vmem, vmem, vmem] + [any_space] * 4,
+        out_specs=[vmem, any_space, any_space, vmem],
         scratch_shapes=[
-            large, large, large,
+            large, large,
             pltpu.VMEM(blocks.shape, jnp.bfloat16),
             pltpu.VMEM((128 * CAP + 1, BLK, BLK), jnp.float32),
             pltpu.VMEM(pivot.shape, jnp.bfloat16),
-            pltpu.VMEM((PIV, NBL * BLK), jnp.bfloat16),
             pltpu.VMEM((PIV, NBL * BLK), jnp.bfloat16),
             pltpu.VMEM((DEPTH, 2, 256, PIV), jnp.bfloat16),
             pltpu.VMEM((256, NBL * BLK), jnp.float32),
@@ -467,50 +473,79 @@
             dma((3,)), dma((8,)), dma((8,)), dma, dma((DEPTH, 2)), dma,
         ],
         compiler_params=pltpu.CompilerParams(
-            collective_id=0, has_side_effects=True, vmem_limit_bytes=62 * 2**20
+            collective_id=0, has_side_effects=True, vmem_limit_bytes=50 * 2**20
         ),
         name="front",
-    )(size, pattern, owner, spots, blocks, front, pivot, panel)[0]
-
-
-PIECES = 8
-
-
-def pass_kernel(source, target, held, in_sem, out_sem):
-    rows = source.shape[0] // PIECES
-    steps = []
-    for i in range(PIECES):
-        part = pl.ds(i * rows, rows)
-        steps.append(
-            (
-                pltpu.make_async_copy(source.at[part], held.at[part], in_sem.at[i]),
-                pltpu.make_async_copy(held.at[part], target.at[part], out_sem.at[i]),
-            )
-        )
-    for take, _ in steps:
-        take.start()
-    for take, give in steps:
-        take.wait()
-        give.start()
-    for _, give in steps:
-        give.wait()
-
-
-def pass_on(array):
+    )(size, pattern, owner, rows_to, cols_to, blocks, front, pivot, panel)
+
+
+def last_kernel(
+    size, pattern, parts, panel_full, factor, out,
+    factor_v, panel_v, lower_v, update0, update1, result, wide0, wide1,
+    load_sem, part_sem, out_sem,
+):
+    g = lax.axis_index("grid")
+    final = (g // 4 + 2) % 4 * 4 + (g % 4 + 2) % 4
+    loads = [
+        pltpu.make_async_copy(factor, factor_v, load_sem.at[0]),
+        pltpu.make_async_copy(panel_full.at[final // 4, final % 4], panel_v, load_sem.at[1]),
+        pltpu.make_async_copy(parts.at[pl.ds(final * 8, 8)], lower_v, load_sem.at[2]),
+    ]
+    for copy in loads:
+        copy.start()
+    passed = []
+    for i in range(1, 16):
+        rows = pl.ds((final + i) % 16 * 8, 8)
+        passed.append(pltpu.make_async_copy(parts.at[rows], out.at[rows], part_sem.at[i - 1]))
+        passed[-1].start()
+    for copy in loads:
+        copy.wait()
+
+    def lower(row, k):
+        return lower_v[2 * (row - final * 4) + k // 2, pl.ds(k % 2 * BLK, BLK), :]
+
+    def write(d, value):
+        result[d - final * 8] = value
+
+    for half, update in ((0, update0), (1, update1)):
+        update[...] = jnp.dot(
+            panel_v[pl.ds(half * 256, 256)], factor_v[...], preferred_element_type=jnp.float32
+        )
+    for half, update in ((0, update0), (1, update1)):
+        first_row = final * 4 + half * 2
+        schur_rows(update, (wide0, wide1), lower, write, pattern, size[0], g, first_row)
+        done = pltpu.make_async_copy(
+            result.at[pl.ds(half * 4, 4)],
+            out.at[pl.ds(final * 8 + half * 4, 4)],
+            out_sem.at[half],
+        )
+        done.start()
+        passed.append(done)
+    for copy in passed:
+        copy.wait()
+
+
+def last_part(size, pattern, parts, panel_full, factor):
     any_space = pl.BlockSpec(memory_space=pl.ANY)
+    smem = pl.BlockSpec(memory_space=pltpu.SMEM)
+    half = pltpu.VMEM((256, NBL * BLK), jnp.float32)
+    wide = pltpu.VMEM((BLK * NBL, BLK), jnp.float32)
+    rows = pltpu.VMEM((8, CAP * BLK, BLK), jnp.bfloat16)
+    dma = pltpu.SemaphoreType.DMA
     return pl.pallas_call(
-        pass_kernel,
-        out_shape=jax.ShapeDtypeStruct(array.shape, array.dtype),
-        in_specs=[any_space],
+        last_kernel,
+        out_shape=jax.ShapeDtypeStruct(parts.shape, parts.dtype),
+        in_specs=[smem, smem] + [any_space] * 3,
         out_specs=any_space,
         scratch_shapes=[
-            pltpu.VMEM(array.shape, array.dtype),
-            pltpu.SemaphoreType.DMA((PIECES,)),
-            pltpu.SemaphoreType.DMA((PIECES,)),
+            pltpu.VMEM(factor.shape, jnp.bfloat16),
+            pltpu.VMEM(panel_full.shape[2:], jnp.bfloat16),
+            rows, half, half, rows, wide, wide,
+            dma((3,)), dma((15,)), dma((2,)),
         ],
-        compiler_params=pltpu.CompilerParams(vmem_limit_bytes=60 * 2**20),
-        name="pass_on",
-    )(array)
+        compiler_params=pltpu.CompilerParams(vmem_limit_bytes=36 * 2**20),
+        name="last_part",
+    )(size, pattern, parts, panel_full, factor)
 
 
 def per_device(
@@ -524,17 +559,20 @@
     pattern,
     front_size,
 ):
-    out = schur_of_front(
+    pattern = pattern[0, :, :, 0].T.reshape(NBL, 1, -1)
+    parts, _, panel_full, factor = front_parts(
         front_size,
-        pattern[0, :, :, 0].T.reshape(NBL, 1, -1),
+        pattern,
         dest_owner.reshape(1, -1),
-        (dest_row * NBL + dest_col).reshape(1, -1),
+        dest_row.reshape(1, -1),
+        dest_col.reshape(1, -1),
         contributions,
         front_entries.reshape(-1, 4, 4, CAP * BLK, BLK),
         pivot_inverse[0],
         panel[0],
     )
-    out = pass_on(out)
+    parts = parts.reshape(-1, CAP * BLK, BLK)
+    out = last_part(front_size, pattern, parts, panel_full, factor)
     return out.reshape(1, -1, NBL, BLK)
 
 

time: 204 us -> 195 us (0.956)
  Pallas kernels: 200 us -> 194 us
    pallas_call x2, Pallas kernels: 200 us -> 194 us  [the longest x1 190 us: front_parts(): pl.pallas_call(front_kernel, out_shape=outs, in_specs=[smem, smem, vmem,...]
where the time goes in v4:
time: 195 us
  Pallas kernels  194 us (99%)
    pallas_call x1, Pallas kernels, front_parts(): pl.pallas_call(front_kernel, out_shape=outs, in_specs=[smem, smem, vmem,...  190 us
    pallas_call x1, Pallas kernels, last_part(): pl.pallas_call(last_kernel, out_shape=jax.ShapeDtypeStruct(parts.shape, p...  4.2 us

profile of v4, /device:TPU:1, one launch (start us, length us, event | category | flops | bytes accessed | tf_op | source)
XLA Modules:
  0.0 194.5 jit_solution(12912832955057498258)
XLA Ops:
  0.7 0.0 copy-start
  0.7 189.7 %front.1 = (bf16[8,4,4,256,128]{4,3,2,1,0:T(8,128)(2,1)S(1)}, bf16[8,4,4,256,128]{4,3,2,1,0:T(8,128)(2,1)}, bf16[4,4,512,1024]{3,2,1,0:T(8,128)(2,1)}, bf16[1024,512]{1,0:T(8,128)(2,1)S(1)}) custom-call(s32[1]{0:T(128)S(6)} %copy.10.size, s32[4,1,64]{2,1,0:T(1,128)} %bitcast.14, s32[1,160]{1,0:T(1,128)} %bitcast.19, s32[1,160]{1,0:T(1,128)} %bitcast.20, ...), custom_call_target="tpu_custom_call" | custom-call | tf_op jit(solution)/shard_map/front/pallas_call | solution.py:451
  190.3 0.0 copy-done
  190.3 4.2 %last_part.1 = bf16[128,256,128]{2,1,0:T(8,128)(2,1)} custom-call(s32[1]{0:T(128)S(6)} %copy.10.size, s32[4,1,64]{2,1,0:T(1,128)S(1)} %bitcast.15, bf16[128,256,128]{2,1,0:T(8,128)(2,1)S(1)} %bitcast.13, bf16[4,4,512,1024]{3,2,1,0:T(8,128)(2,1)} %get-tuple-element.9.panel_full, bf16[1024,512]{1,0:T(8,128)(2,1)S(1)} %get-tuple-element.10.factor), custom_call_target="tpu_custom_call" | custom-call | tf_op jit(solution)/shard_map/last_part/pallas_call | solution.py:535
Async XLA Ops:
  0.7 189.7 %copy-start = (s32[1,64,4,1]{1,3,2,0:T(1,128)S(1)}, s32[1,64,4,1]{1,3,2,0:T(1,128)}, u32[]{:S(2)}) copy-start(s32[1,64,4,1]{1,3,2,0:T(1,128)} %param.16) | copy-start | bytes 3076

commit v5 on v4

--- a/solution.py
+++ b/solution.py
@@ -361,7 +361,6 @@
 
     pl.semaphore_wait(barrier, 13)
     first_line()
-    second_line(0)
     load_pivot.start()
     make_slots()
     start(3, 0)
@@ -369,6 +368,7 @@
     lax.fori_loop(0, 128, fill, 0)
     for part in range(3):
         start(part, 0)
+    second_line(0)
     finish(3, 0)
     start(3, 1)
     for part in range(3):

time: 195 us -> 192 us (0.985)
  Pallas kernels: 194 us -> 191 us
    pallas_call x1, Pallas kernels: 190 us -> 187 us  [front_parts(): pl.pallas_call(front_kernel, out_shape=outs, in_specs=[smem, smem, vmem,...]
where the time goes in v5:
time: 192 us
  Pallas kernels  191 us (99%)
    pallas_call x1, Pallas kernels, front_parts(): pl.pallas_call(front_kernel, out_shape=outs, in_specs=[smem, smem, vmem,...  187 us
    pallas_call x1, Pallas kernels, last_part(): pl.pallas_call(last_kernel, out_shape=jax.ShapeDtypeStruct(parts.shape, p...  4.2 us

profile of v5, /device:TPU:1, one launch (start us, length us, event | category | flops | bytes accessed | tf_op | source)
XLA Modules:
  0.0 191.5 jit_solution(2877994551823972649)
XLA Ops:
  0.7 0.0 copy-start
  0.7 186.6 %front.1 = (bf16[8,4,4,256,128]{4,3,2,1,0:T(8,128)(2,1)S(1)}, bf16[8,4,4,256,128]{4,3,2,1,0:T(8,128)(2,1)}, bf16[4,4,512,1024]{3,2,1,0:T(8,128)(2,1)}, bf16[1024,512]{1,0:T(8,128)(2,1)S(1)}) custom-call(s32[1]{0:T(128)S(6)} %copy.10.size, s32[4,1,64]{2,1,0:T(1,128)} %bitcast.14, s32[1,160]{1,0:T(1,128)} %bitcast.19, s32[1,160]{1,0:T(1,128)} %bitcast.20, ...), custom_call_target="tpu_custom_call" | custom-call | tf_op jit(solution)/shard_map/front/pallas_call | solution.py:451
  187.3 0.0 copy-done
  187.3 4.2 %last_part.1 = bf16[128,256,128]{2,1,0:T(8,128)(2,1)} custom-call(s32[1]{0:T(128)S(6)} %copy.10.size, s32[4,1,64]{2,1,0:T(1,128)S(1)} %bitcast.15, bf16[128,256,128]{2,1,0:T(8,128)(2,1)S(1)} %bitcast.13, bf16[4,4,512,1024]{3,2,1,0:T(8,128)(2,1)} %get-tuple-element.9.panel_full, bf16[1024,512]{1,0:T(8,128)(2,1)S(1)} %get-tuple-element.10.factor), custom_call_target="tpu_custom_call" | custom-call | tf_op jit(solution)/shard_map/last_part/pallas_call | solution.py:535
Async XLA Ops:
  0.7 186.7 %copy-start = (s32[1,64,4,1]{1,3,2,0:T(1,128)S(1)}, s32[1,64,4,1]{1,3,2,0:T(1,128)}, u32[]{:S(2)}) copy-start(s32[1,64,4,1]{1,3,2,0:T(1,128)} %param.16) | copy-start | bytes 3076

commit v6 on v5

--- a/solution.py
+++ b/solution.py
@@ -64,7 +64,7 @@
             return ((f // 2 + d // 2) % 4) * 2 + (f + d) % 2
         return (me[axis] + d) % 4
 
-    offsets = ((2, 6, 4, 3, 7, 5, 1), (1, 3, 2), (1, 3, 2))
+    offsets = ((4, 5, 2, 6, 3, 7, 1), (2, 1, 3), (2, 1, 3))
 
     barrier = pltpu.get_barrier_semaphore()
     for axis in range(3):
@@ -91,24 +91,25 @@
         second = jnp.max(jnp.where(match, block, -1), axis=1, keepdims=True)
         nowhere = front.shape[0] * 16 * CAP
         square = (128, BLK)
+        lane = lax.broadcasted_iota(jnp.int32, square, 1)
+        hits = []
         for j, (chosen, there) in enumerate(
             ((first, second >= 0), (second, second > first))
         ):
             hit = jnp.max(jnp.where(block == chosen, spot, 0), axis=1, keepdims=True)
             hit = jnp.where(there, hit, nowhere)
-            places[pl.ds(j, 128, stride=CAP), :] = jnp.broadcast_to(hit, square)
+            hits.append(jnp.broadcast_to(hit, square))
             index = jnp.broadcast_to(jnp.where(there, chosen, 0), square)
-            diagonal = lax.broadcasted_iota(jnp.int32, square, 0) == lax.broadcasted_iota(
-                jnp.int32, square, 1
-            )
+            diagonal = lax.broadcasted_iota(jnp.int32, square, 0) == lane
             chain_v[j : j + 1, :] = jnp.sum(
                 jnp.where(diagonal, index, 0), axis=0, keepdims=True
             )
         copy = pltpu.make_async_copy(chain_v, chain, chain_sem)
         copy.start()
+        places[pl.ds(0, 128), :] = jnp.where(lane < BLK // CAP, *hits)
 
         def spread(d, carry):
-            m0[d // 16, (d // 4) % 4, d % 4] = places[pl.ds(d * CAP, CAP), :]
+            m0[d // 16, (d // 4) % 4, d % 4] = places[pl.ds(d, 1), :]
             return carry
 
         lax.fori_loop(0, 128, spread, 0)
@@ -216,10 +217,15 @@
 
     def make_tables():
         def spread(d, carry):
-            places[pl.ds(d * CAP, CAP), :] = m3[d // 16, (d // 4) % 4, d % 4]
+            places[pl.ds(d, 1), :] = m3[d // 16, (d // 4) % 4, d % 4]
             return carry
 
         lax.fori_loop(0, 128, spread, 0)
+        both = places[pl.ds(0, 128), :]
+        part = lax.broadcasted_iota(jnp.int32, both.shape, 1) // (BLK // CAP)
+        for j in range(CAP):
+            mine = jnp.max(jnp.where(part == j, both, 0), axis=1, keepdims=True)
+            places[pl.ds(j, 128, stride=CAP), :] = jnp.broadcast_to(mine, both.shape)
         where = places[...]
         slot = lax.broadcasted_iota(jnp.int32, where.shape, 0)
         lane = lax.broadcasted_iota(jnp.int32, where.shape, 1)
@@ -446,7 +452,7 @@
         jax.ShapeDtypeStruct((4, 4) + panel.shape, jnp.bfloat16),
         pltpu.VMEM((PIV, NBL * BLK), jnp.bfloat16),
     ]
-    small = pltpu.VMEM(grid_of + (CAP, BLK), jnp.int32)
+    small = pltpu.VMEM(grid_of + (1, BLK), jnp.int32)
     large = pltpu.VMEM(grid_of + (CAP * BLK, BLK), jnp.bfloat16)
     return pl.pallas_call(
         front_kernel,
@@ -488,8 +494,14 @@
     final = (g // 4 + 2) % 4 * 4 + (g % 4 + 2) % 4
     loads = [
         pltpu.make_async_copy(factor, factor_v, load_sem.at[0]),
-        pltpu.make_async_copy(panel_full.at[final // 4, final % 4], panel_v, load_sem.at[1]),
-        pltpu.make_async_copy(parts.at[pl.ds(final * 8, 8)], lower_v, load_sem.at[2]),
+        pltpu.make_async_copy(parts.at[pl.ds(final * 8, 8)], lower_v, load_sem.at[1]),
+    ] + [
+        pltpu.make_async_copy(
+            panel_full.at[final // 4, final % 4, pl.ds(half * 256, 256)],
+            panel_v.at[pl.ds(half * 256, 256)],
+            load_sem.at[2 + half],
+        )
+        for half in (0, 1)
     ]
     for copy in loads:
         copy.start()
@@ -498,7 +510,7 @@
         rows = pl.ds((final + i) % 16 * 8, 8)
         passed.append(pltpu.make_async_copy(parts.at[rows], out.at[rows], part_sem.at[i - 1]))
         passed[-1].start()
-    for copy in loads:
+    for copy in loads[:2]:
         copy.wait()
 
     def lower(row, k):
@@ -508,10 +520,10 @@
         result[d - final * 8] = value
 
     for half, update in ((0, update0), (1, update1)):
+        loads[2 + half].wait()
         update[...] = jnp.dot(
             panel_v[pl.ds(half * 256, 256)], factor_v[...], preferred_element_type=jnp.float32
         )
-    for half, update in ((0, update0), (1, update1)):
         first_row = final * 4 + half * 2
         schur_rows(update, (wide0, wide1), lower, write, pattern, size[0], g, first_row)
         done = pltpu.make_async_copy(
@@ -541,7 +553,7 @@
             pltpu.VMEM(factor.shape, jnp.bfloat16),
             pltpu.VMEM(panel_full.shape[2:], jnp.bfloat16),
             rows, half, half, rows, wide, wide,
-            dma((3,)), dma((15,)), dma((2,)),
+            dma((4,)), dma((15,)), dma((2,)),
         ],
         compiler_params=pltpu.CompilerParams(vmem_limit_bytes=36 * 2**20),
         name="last_part",

time: 192 us -> 191 us (level)
  no operation moved by 1% of the time
where the time goes in v6:
time: 191 us
  Pallas kernels  190 us (99%)
    pallas_call x1, Pallas kernels, front_parts(): pl.pallas_call(front_kernel, out_shape=outs, in_specs=[smem, smem, vmem,...  186 us
    pallas_call x1, Pallas kernels, last_part(): pl.pallas_call(last_kernel, out_shape=jax.ShapeDtypeStruct(parts.shape, p...  4.15 us

profile of v6, /device:TPU:1, one launch (start us, length us, event | category | flops | bytes accessed | tf_op | source)
XLA Modules:
  0.0 190.7 jit_solution(2426938687927122315)
XLA Ops:
  0.7 0.0 copy-start
  0.7 185.9 %front.1 = (bf16[8,4,4,256,128]{4,3,2,1,0:T(8,128)(2,1)S(1)}, bf16[8,4,4,256,128]{4,3,2,1,0:T(8,128)(2,1)}, bf16[4,4,512,1024]{3,2,1,0:T(8,128)(2,1)}, bf16[1024,512]{1,0:T(8,128)(2,1)S(1)}) custom-call(s32[1]{0:T(128)S(6)} %copy.10.size, s32[4,1,64]{2,1,0:T(1,128)} %bitcast.14, s32[1,160]{1,0:T(1,128)} %bitcast.19, s32[1,160]{1,0:T(1,128)} %bitcast.20, ...), custom_call_target="tpu_custom_call" | custom-call | tf_op jit(solution)/shard_map/front/pallas_call | solution.py:457
  186.5 0.0 copy-done
  186.5 4.2 %last_part.1 = bf16[128,256,128]{2,1,0:T(8,128)(2,1)} custom-call(s32[1]{0:T(128)S(6)} %copy.10.size, s32[4,1,64]{2,1,0:T(1,128)S(1)} %bitcast.15, bf16[128,256,128]{2,1,0:T(8,128)(2,1)S(1)} %bitcast.13, bf16[4,4,512,1024]{3,2,1,0:T(8,128)(2,1)} %get-tuple-element.9.panel_full, bf16[1024,512]{1,0:T(8,128)(2,1)S(1)} %get-tuple-element.10.factor), custom_call_target="tpu_custom_call" | custom-call | tf_op jit(solution)/shard_map/last_part/pallas_call | solution.py:547
Async XLA Ops:
  0.7 185.9 %copy-start = (s32[1,64,4,1]{1,3,2,0:T(1,128)S(1)}, s32[1,64,4,1]{1,3,2,0:T(1,128)}, u32[]{:S(2)}) copy-start(s32[1,64,4,1]{1,3,2,0:T(1,128)} %param.16) | copy-start | bytes 3076
